TPU v7x, 512 devices: a whole 4x8x8 slice. The times are simulated.
512 devices in a mesh: dp: 32 (over z, y_hi), tensor: 16 (over x, y_lo, core).
Axes of the slice: x: 4, y: 8 (y_hi: 4, y_lo: 2; y = y_hi * 2 + y_lo), z: 8, core: 2. Of those that a mesh axis runs over, the one named last changes fastest.
Arguments:
- hidden: bfloat16 [4096, 8192], P('dp', 'tensor'), may hold values from -27 to 27
- gain: bfloat16 [8192], P('tensor'), may hold values from 0.5 to 1.5
- proj_weight: bfloat16 [8192, 4096], P('dp', 'tensor'), may hold values from -0.0625 to 0.0625
- b_c: bfloat16 [4096, 4096], P('dp', 'tensor'), may hold values from -4 to 4
- ssm_x: bfloat16 [4096, 16384], P('dp', 'tensor'), may hold values from -4 to 4
- dy: bfloat16 [4096, 16384], P('dp', 'tensor'), may hold values from -0.015625 to 0.015625
- log_decay: float32 [4096, 256], P('dp', 'tensor'), may hold values from -0.75 to 0
Outputs:
- input_grad: bfloat16 [4096, 8192], P('dp', 'tensor')
- weight_grad: bfloat16 [8192, 4096], P('dp', 'tensor')
All inputs are finite; a program needn't handle non-finite values.
Results may differ from a plain program's by a relative error of at most 0.025.
Values may be sent and summed in bfloat16 or wider, within the bound.
A program may use at most 64 MiB of HBM per device.

v0:
```python
import math

import jax
import jax.numpy as jnp
from jax import lax
from jax.sharding import PartitionSpec as P

MHEAD = 64


EPSILON = 1e-05


def swapped(value, axis, apart):
    mask = 2**apart
    pairs = [(source, source ^ mask) for source in range(lax.axis_size(axis))]
    return lax.ppermute(value, axis, pairs)


def shards(hidden, gain, proj_weight, b_c, ssm_x, dy, log_decay):
    length = hidden.shape[0]
    own_width = hidden.shape[1]
    n_data = lax.axis_size("dp")
    half_width = b_c.shape[1] // 2
    b_own = b_c[:, :half_width].astype(jnp.float32)
    c_own = b_c[:, half_width:].astype(jnp.float32)
    causal = lax.broadcasted_iota(jnp.int32, (length, length), 0) >= lax.broadcasted_iota(
        jnp.int32, (length, length), 1
    )
    mamba_count = ssm_x.shape[1] // MHEAD
    input_heads = ssm_x.reshape(length, mamba_count, MHEAD)
    grad_heads = dy.reshape(length, mamba_count, MHEAD)
    inner_prod = jnp.einsum(
        "thd,shd->hts", grad_heads, input_heads, preferred_element_type=jnp.float32
    )
    running = jnp.cumsum(log_decay, axis=0).T
    log_gap = running[:, :, None] - running[:, None, :]
    decays = jnp.exp(jnp.where(causal[None], log_gap, -jnp.inf))
    gram_part = jnp.sum(inner_prod * decays, axis=0)
    gram_other = swapped(gram_part.astype(jnp.bfloat16), "tensor", 0).astype(gram_part.dtype)
    gram_total = gram_part + gram_other
    grad_b = jnp.dot(gram_total.T, c_own, precision=lax.Precision.HIGHEST)
    grad_c = jnp.dot(gram_total, b_own, precision=lax.Precision.HIGHEST)
    group_grad = jnp.concatenate([grad_b, grad_c], axis=1)
    dproj = group_grad.astype(jnp.bfloat16)
    full_hidden, full_gain = (
        lax.all_gather(hidden, "tensor", axis=1, tiled=True),
        lax.all_gather(gain, "tensor", axis=0, tiled=True),
    )
    hidden_f = full_hidden.astype(jnp.float32)
    root_mean = jnp.sqrt(jnp.mean(hidden_f * hidden_f, axis=-1, keepdims=True) + EPSILON)
    unit_rows = hidden_f / root_mean
    gain_f = full_gain.astype(jnp.float32)
    normed = (unit_rows * gain_f).astype(jnp.bfloat16)
    inv_root = 1.0 / math.sqrt(length * n_data)
    weight_grad = lax.psum_scatter(
        (
            lax.dot_general(
                normed, dproj, (((0,), (0,)), ((), ())), preferred_element_type=jnp.float32
            )
            * inv_root
        ).astype(jnp.bfloat16),
        "dp",
        scatter_dimension=0,
        tiled=True,
    )
    partial_grad = lax.dot_general(
        dproj,
        lax.all_gather(proj_weight, "dp", axis=0, tiled=True),
        (((1,), (1,)), ((), ())),
        preferred_element_type=jnp.float32,
    )
    first_col = lax.axis_index("tensor") * own_width
    unit_own = lax.dynamic_slice_in_dim(unit_rows, first_col, own_width, 1)
    dnormed = lax.psum(partial_grad.astype(jnp.bfloat16), "tensor").astype(jnp.float32)
    scaled = gain_f * dnormed
    mean_term = jnp.mean(scaled * unit_rows, axis=-1, keepdims=True)
    scaled_own = lax.dynamic_slice_in_dim(scaled, first_col, own_width, 1)
    input_grad = ((scaled_own - unit_own * mean_term) / root_mean).astype(jnp.bfloat16)
    return (input_grad, weight_grad)


def solution(mesh):
    return jax.shard_map(
        shards,
        mesh=mesh,
        in_specs=(
            P("dp", "tensor"),
            P("tensor"),
            P("dp", "tensor"),
            P("dp", "tensor"),
            P("dp", "tensor"),
            P("dp", "tensor"),
            P("dp", "tensor"),
        ),
        out_specs=(P("dp", "tensor"), P("dp", "tensor")),
        check_vma=False,
    )
```

profile of v0, /device:TPU:1, one launch (start us, length us, event | category | flops | bytes accessed | tf_op | source)
XLA Modules:
  0.0 533.9 jit_solution(12353529414137322717)
XLA Ops:
  7.2 0.0 all-gather.4.cloned.1.call-start
  7.2 0.7 all-gather.4.cloned.1.call-update
  7.9 0.0 all-gather.6.cloned.1.call-start
  7.9 0.7 all-gather.6.cloned.1.call-update
  8.6 0.0 all-reduce.2.cloned.1.call-start
  8.7 1.1 copy.19
  9.8 1.1 copy.20
  10.9 0.8 copy.21
  11.7 0.2 reduce_window_sum.11
  11.9 0.1 copy.22
  12.0 0.5 fusion.3
  12.6 8.8 %collective-permute-start = (bf16[128,128]{1,0:T(8,128)(2,1)S(1)}, bf16[128,128]{1,0:T(8,128)(2,1)S(1)}, u32[]{:S(2)}, u32[]{:S(2)}) collective-permute-start(bf16[128,128]{1,0:T(8,128)(2,1)S(1)} %convert_element_type.31), channel_id=1, source_target_pairs={{0,1},{1,0},{2,3},{3,2},{4,5},{5,4},{6,7},{7,6},{8,9},{9,8},{10,11... | collective-permute-start | bytes 98312 | tf_op jit(solution)/shard_map/ppermute | solution.py:17
  21.4 0.8 collective-permute-done
  22.2 1.0 convolution_convert_fusion.2
  23.2 1.0 convolution_convert_fusion.1
  24.2 0.0 copy-start.1
  24.2 93.1 %all-gather.4.cloned.1.call-done = bf16[8192,256]{1,0:T(8,128)(2,1)} async-done(((bf16[256,256]{1,0:T(8,128)(2,1)}), bf16[8192,256]{1,0:T(8,128)(2,1)}) %all-gather.4.cloned.1.call-update) | async-done | bytes 4194320 | tf_op jit(solution)/shard_map/all_gather | solution.py:69
  117.3 5.1 convolution_convert_fusion
  122.4 0.0 all-reduce.2.cloned.1.call-update
  122.4 0.0 reduce-scatter.2.cloned.1.call-start
  122.5 0.0 copy-done.1
  122.5 21.3 %all-gather = bf16[16,1,512]{2,1,0:T(2,128)(2,1)S(1)} all-gather(bf16[1,1,512]{2,1,0:T(2,128)(2,1)S(1)} %reshape.34), channel_id=1, replica_groups=mesh['dp'=32,'tensor'=16] {'tensor'}, dimensions={0}, use_global_device_ids=true | all-gather | bytes 17408 | tf_op jit(solution)/shard_map/all_gather | solution.py:48
  143.8 13.4 %all-gather.6.cloned.1.call-done = bf16[128,8192]{1,0:T(8,128)(2,1)} async-done(((bf16[128,512]{1,0:T(8,128)(2,1)}), bf16[128,8192]{1,0:T(8,128)(2,1)}) %all-gather.6.cloned.1.call-update) | async-done | bytes 2097168 | tf_op jit(solution)/shard_map/all_gather | solution.py:47
  157.2 2.1 fusion.1
  159.2 4.9 fusion
  164.2 0.0 copy-start
  164.2 0.0 reduce-scatter.2.cloned.1.call-update
  164.2 130.1 %all-reduce.2.cloned.1.call-done = bf16[128,8192]{1,0:T(8,128)(2,1)} async-done(((bf16[128,8192]{1,0:T(8,128)(2,1)}), bf16[128,8192]{1,0:T(8,128)(2,1)}) %all-reduce.2.cloned.1.call-update) | async-done | bytes 2097168 | tf_op jit(solution)/shard_map/psum | solution.py:75
  294.4 0.0 copy-done
  294.4 2.5 multiply_reduce_fusion
  296.9 0.8 divide_convert_fusion
  297.7 229.6 %reduce-scatter.2.cloned.1.call-done = bf16[256,256]{1,0:T(8,128)(2,1)} async-done(((bf16[8192,256]{1,0:T(8,128)(2,1)}), bf16[256,256]{1,0:T(8,128)(2,1)}) %reduce-scatter.2.cloned.1.call-update) | async-done | bytes 131088 | tf_op jit(solution)/shard_map/reduce_scatter | solution.py:56
  (6 shorter events, 0.1 us)
Async XLA Ops:
  7.2 110.2 %all-gather.4.cloned.1.call-start = ((), (), s32[]{:S(2)}) async-start(), calls=%async_computation.1 | async-start | bytes 4325376 | tf_op jit(solution)/shard_map/all_gather | solution.py:69
  7.9 149.3 %all-gather.6.cloned.1.call-start = ((), (), s32[]{:S(2)}) async-start(), calls=%async_computation.3 | async-start | bytes 2228224 | tf_op jit(solution)/shard_map/all_gather | solution.py:47
  8.6 285.7 %all-reduce.2.cloned.1.call-start = ((), (), s32[]{:S(2)}) async-start(), calls=%async_computation.2 | async-start | bytes 4194304 | tf_op jit(solution)/shard_map/psum | solution.py:75
  12.6 9.6 %collective-permute-start = (bf16[128,128]{1,0:T(8,128)(2,1)S(1)}, bf16[128,128]{1,0:T(8,128)(2,1)S(1)}, u32[]{:S(2)}, u32[]{:S(2)}) collective-permute-start(bf16[128,128]{1,0:T(8,128)(2,1)S(1)} %convert_element_type.31), channel_id=1, source_target_pairs={{0,1},{1,0},{2,3},{3,2},{4,5},{5,4},{6,7},{7,6},{8,9},{9,8},{10,11... | collective-permute-start | bytes 98312 | tf_op jit(solution)/shard_map/ppermute | solution.py:17
  24.2 98.3 %copy-start.1 = (bf16[512]{0:T(512)(128)(2,1)S(1)}, bf16[512]{0:T(512)(128)(2,1)}, u32[]{:S(2)}) copy-start(bf16[512]{0:T(512)(128)(2,1)} %param.8) | copy-start | bytes 3076
  122.4 404.9 %reduce-scatter.2.cloned.1.call-start = ((), (), s32[]{:S(2)}) async-start(), calls=%async_computation.4 | async-start | bytes 4325376 | tf_op jit(solution)/shard_map/reduce_scatter | solution.py:56
  164.2 130.2 %copy-start = (bf16[128,8192]{1,0:T(8,128)(2,1)S(1)}, bf16[128,8192]{1,0:T(8,128)(2,1)}, u32[]{:S(2)}) copy-start(bf16[128,8192]{1,0:T(8,128)(2,1)} %all-gather.6.cloned.1.call-done) | copy-start | bytes 6291460
Sparse Core Ops, SparseCore 0:
  11.2 106.1 all-gather.3
  119.4 37.6 all-gather.5
  160.1 134.2 all-reduce.1
  299.3 228.0 reduce-scatter.1
where the time goes:
time: 538 us; the launch traced here: 534 us
  waiting for transfers between devices  469 us (87%)
  blocking collectives  21.3 us (4%)
  between operations  13.9 us (3%)
  matrix products  12.5 us (2%)
  starting transfers between devices  8.94 us (2%)
  other arithmetic  5.66 us (1%)
    reduce_scatter x1, waiting for transfers between devices, shards(): lax.psum_scatter((lax.dot_general(normed, dproj, (((0,), (0,)), ((), ()))...  230 us
    psum x1, waiting for transfers between devices, shards(): lax.psum(partial_grad.astype(jnp.bfloat16), 'tensor').astype(jnp.float32)  130 us
    all_gather x1, waiting for transfers between devices, shards(): lax.all_gather(proj_weight, 'dp', axis=0, tiled=True)  93.1 us
    all_gather x1, blocking collectives, shards(): lax.all_gather(gain, 'tensor', axis=0, tiled=True)  21.3 us
    all_gather x1, waiting for transfers between devices, shards(): lax.all_gather(hidden, 'tensor', axis=1, tiled=True)  13.4 us
  transfers between devices with their start and end apart: 5, of which 5 were waited for; matrix products, arithmetic and copies ran while one was open for 4% of the time, Pallas kernels for 0%

commit v1 on v0

v1 whole, which is shorter than its diff:
```python
import jax
import jax.numpy as jnp
from jax import lax
from jax.experimental import pallas as pl
from jax.experimental.pallas import tpu as pltpu
from jax.sharding import PartitionSpec as P

MHEAD = 64
EPSILON = 1e-05
MESH = pl.DeviceIdType.MESH
F32 = jnp.float32
BF16 = jnp.bfloat16
HIGHEST = lax.Precision.HIGHEST


def device(za, zb, yh, x, yl, c):
    return {"dp": (za * 2 + zb) * 4 + yh, "tensor": x * 4 + yl * 2 + c}


def nt_dot(a, b, precision=None):
    return lax.dot_general(
        a, b, (((1,), (1,)), ((), ())), preferred_element_type=F32, precision=precision
    )


def nn_dot(a, b, precision=None):
    return lax.dot_general(
        a, b, (((1,), (0,)), ((), ())), preferred_element_type=F32, precision=precision
    )


class Slots:
    def __init__(self):
        self.count = 0

    def take(self, n):
        first = self.count
        self.count += n
        return first


SLOTS = Slots()
S_HID = SLOTS.take(4)
S_HAG = SLOTS.take(8)
S_W = SLOTS.take(8)
S_SQ = SLOTS.take(9)
S_GRAM = SLOTS.take(1)
S_DY = SLOTS.take(4)
S_DZ = SLOTS.take(4)
S_DC = SLOTS.take(8)
S_P = SLOTS.take(8)
S_Q = SLOTS.take(4)
S_G = SLOTS.take(8)
S_MEAN = SLOTS.take(9)
N_SLOTS = SLOTS.count


def kernel(
    hid_ref,
    gain_ref,
    w_ref,
    bc_ref,
    x_ref,
    dy_ref,
    ld_ref,
    igrad_ref,
    wgrad_ref,
    ht,
    hall,
    wall,
    sums,
    sums_in,
    gram,
    dall,
    psend,
    precv,
    rsum,
    qrecv,
    gsend,
    grecv,
    ssem,
    rsem,
    lsem,
):
    dp = lax.axis_index("dp")
    ten = lax.axis_index("tensor")
    z, yh = dp // 4, dp % 4
    za, zb = z // 2, z % 2
    x, yl, c = ten // 4, (ten // 2) % 2, ten % 2
    me = (za, zb, yh, x, yl, c)

    def remote(src, dst, slot, dev, rslot=None):
        rslot = slot if rslot is None else rslot
        return pltpu.make_async_remote_copy(
            src_ref=src,
            dst_ref=dst,
            send_sem=ssem.at[slot],
            recv_sem=rsem.at[rslot],
            device_id=device(*dev),
            device_id_type=MESH,
        )

    sibling = (za, zb, yh, x, yl, 1 - c)
    plane = [(dx, fy) for dx in range(4) for fy in range(2) if dx or fy]
    plane.sort(key=lambda o: (o[0] == 2, o[0] != 0))

    def plane_dev(dx, fy):
        return (za, zb, yh, (x + dx) % 4, (yl + fy) % 2, c)

    def plane_src(dx, fy):
        return (x + 4 - dx) % 4, (yl + fy) % 2

    def far(dza, fc):
        return ((za + dza) % 4, zb, yh, x, yl, (c + fc) % 2)

    depth = [(dza, fc) for dza in (2, 1, 3) for fc in range(2)] + [(0, 1)]

    def hid_target(i, h):
        return (za, yl, 2 * c + i, x, zb, h)

    def hid_target_is_me(i, h):
        return (yl == zb) & (yh == 2 * c + i) & (c == h)

    def hid_source(ys):
        return (za, yl, ys, x, zb, yh // 2)

    def hid_source_is_me(ys):
        return (yl == zb) & (ys == yh) & (c == yh // 2)

    barrier = pltpu.get_barrier_semaphore()

    def greet(dev):
        pl.semaphore_signal(barrier, inc=1, device_id=device(*dev), device_id_type=MESH)

    greet(sibling)
    for dx, fy in plane:
        greet(plane_dev(dx, fy))
    for dy in range(1, 4):
        greet((za, zb, (yh + dy) % 4, x, yl, c))
    greet((za, 1 - zb, yh, x, yl, c))
    for dza, fc in depth[:-1]:
        greet(far(dza, fc))
    met = 1 + 7 + 3 + 1 + 6
    for i in range(2):
        for h in range(2):

            @pl.when(jnp.logical_not(hid_target_is_me(i, h)))
            def _():
                greet(hid_target(i, h))

    for ys in range(4):

        @pl.when(jnp.logical_not(hid_source_is_me(ys)))
        def _():
            greet(hid_source(ys))

    own_hop = jnp.where((yl == zb) & (c == yh // 2), 1, 0)

    hid = hid_ref[...].astype(F32)
    gain = gain_ref[...].astype(F32)
    scaled = hid * gain
    for k in range(4):
        ht[k] = scaled[:, k * 128 : (k + 1) * 128].T.astype(BF16)

    def row_of(column):
        return jnp.broadcast_to(column, (128, 128)).T[0:8, :]

    def column_of(row):
        return jnp.broadcast_to(row[0:1, :], (128, 128)).T

    sums[0, 0] = row_of(jnp.sum(hid * hid, axis=1, keepdims=True))
    wall[c, za] = w_ref[pl.ds(pl.multiple_of(c * 128, 128), 128), :]

    pl.semaphore_wait(barrier, met + 8 - 2 * own_hop)

    def hid_copy(i, h):
        return remote(
            ht.at[2 * i + h],
            hall.at[zb, x, :, pl.ds(pl.multiple_of(yh * 128, 128), 128)],
            S_HID + 2 * i + h,
            hid_target(i, h),
            S_HID + yh,
        )

    def hid_arrival(ys):
        return remote(
            ht.at[0], hall.at[yl, x, :, ys * 128 : (ys + 1) * 128], S_HID + ys, sibling
        )

    for i in range(2):
        for h in range(2):

            @pl.when(jnp.logical_not(hid_target_is_me(i, h)))
            def _():
                hid_copy(i, h).start()

            @pl.when(hid_target_is_me(i, h))
            def _():
                own = pltpu.make_async_copy(
                    ht.at[2 * i + h],
                    hall.at[yl, x, :, pl.ds(pl.multiple_of(yh * 128, 128), 128)],
                    lsem,
                )
                own.start()
                own.wait()

    def sum_sibling(which, base):
        return remote(sums.at[which, 0], sums_in.at[which, 0], base, sibling)

    def sum_plane(which, base, n, dx, fy):
        return remote(
            sums.at[which, 1], sums_in.at[which, 1 + n], base + 1 + n, plane_dev(dx, fy)
        )

    sum_sibling(0, S_SQ).start()

    def w_copy(n, dza, fc):
        core = (c + fc) % 2
        return remote(
            w_ref.at[pl.ds(pl.multiple_of(core * 128, 128), 128), :],
            wall.at[c, za],
            S_W + n,
            far(dza, fc),
        )

    def w_arrival(n, dza, fc):
        return remote(
            w_ref.at[0:128, :], wall.at[(c + fc) % 2, (za + 4 - dza) % 4], S_W + n, sibling
        )

    for n, (dza, fc) in enumerate(depth):
        w_copy(n, dza, fc).start()

    rows = lax.broadcasted_iota(jnp.int32, (128, 128), 0)
    cols = lax.broadcasted_iota(jnp.int32, (128, 128), 1)
    causal = rows >= cols
    heads = ld_ref.shape[1]
    padded = jnp.concatenate([ld_ref[...], jnp.zeros((128, 128 - heads), F32)], axis=1)
    running = nn_dot(causal.astype(F32), padded, HIGHEST)
    running_t = running.T
    low = cols < MHEAD
    total = jnp.zeros((128, 128), F32)
    for p in range(heads // 2):
        xp = x_ref[:, p * 128 : (p + 1) * 128]
        zero = jnp.zeros_like(xp)
        both = jnp.concatenate([jnp.where(low, xp, zero), jnp.where(low, zero, xp)], axis=0)
        inner = nt_dot(dy_ref[:, p * 128 : (p + 1) * 128], both)
        for k in range(2):
            h = 2 * p + k
            gap = running[:, h : h + 1] - running_t[h : h + 1, :]
            decay = jnp.exp(jnp.where(causal, gap, -1e30))
            total = total + inner[:, k * 128 : (k + 1) * 128] * decay
    gram[0] = total
    gram_copy = remote(gram.at[0], gram.at[1], S_GRAM, sibling)
    gram_copy.start()

    sum_sibling(0, S_SQ).wait_recv()
    sums[0, 1] = sums[0, 0] + sums_in[0, 0]
    for n, (dx, fy) in enumerate(plane):
        sum_plane(0, S_SQ, n, dx, fy).start()

    gram_copy.wait_recv()
    total = gram[0] + gram[1]
    bc = bc_ref[...].astype(F32)
    grad_b = nn_dot(total.T, bc[:, 128:], HIGHEST)
    grad_c = nn_dot(total, bc[:, :128], HIGHEST)

    for n, (dx, fy) in enumerate(plane):
        sum_plane(0, S_SQ, n, dx, fy).wait_recv()
    square = sums[0, 1]
    for n in range(7):
        square = square + sums_in[0, 1 + n]
    mean_square = column_of(square) * (1.0 / 8192.0) + EPSILON
    inv_root = lax.rsqrt(mean_square)
    dall[c, zb, yh] = jnp.concatenate([grad_b * inv_root, grad_c * inv_root], axis=1).astype(BF16)

    def d_y(dy):
        block = dall.at[c, zb, yh]
        return remote(block, block, S_DY + dy, (za, zb, (yh + dy) % 4, x, yl, c))

    def d_z(dy):
        block = dall.at[c, zb, (yh + 4 - dy) % 4]
        return remote(block, block, S_DZ + dy, (za, 1 - zb, yh, x, yl, c))

    def d_c(k, dy):
        block = dall.at[c, (zb + k) % 2, (yh + 4 - dy) % 4]
        return remote(block, block, S_DC + 4 * k + dy, sibling)

    for dy in (2, 1, 3):
        d_y(dy).start()
    d_z(0).start()
    d_c(0, 0).start()

    def h_copy(n, dx, fy):
        block = hall.at[yl, x]
        return remote(block, block, S_HAG + n, plane_dev(dx, fy))

    def h_arrival(n, dx, fy):
        sx, sy = plane_src(dx, fy)
        return remote(hall.at[sy, sx], hall.at[sy, sx], S_HAG + n, sibling)

    for ys in range(4):

        @pl.when(jnp.logical_not(hid_source_is_me(ys)))
        def _():
            hid_arrival(ys).wait_recv()

    for n, (dx, fy) in enumerate(plane):
        h_copy(n, dx, fy).start()

    for dy in (1, 3, 2):
        d_y(dy).wait_recv()
        d_z(dy).start()
        d_c(0, dy).start()

    for n, (dza, fc) in enumerate(depth):
        w_arrival(n, dza, fc).wait_recv()

    def p_copy(n, dx, fy):
        tx, ty = (x + dx) % 4, (yl + fy) % 2
        return remote(psend.at[ty, tx], precv.at[yl, x], S_P + n, plane_dev(dx, fy))

    def p_arrival(n, dx, fy):
        sx, sy = plane_src(dx, fy)
        return remote(psend.at[sy, sx], precv.at[sy, sx], S_P + n, sibling)

    def terms(k):
        side = (zb + k) % 2
        for ys in range(4):
            out = nt_dot(dall[0, side, ys], wall[0].reshape(512, 256))
            out = out + nt_dot(dall[1, side, ys], wall[1].reshape(512, 256))
            for tx in range(4):
                psend[side, tx, ys * 128 : (ys + 1) * 128, :] = out[
                    :, tx * 128 : (tx + 1) * 128
                ].astype(BF16)

        @pl.when(side == yl)
        def _():
            for n, (dx, fy) in enumerate(plane):
                if fy == 0:
                    p_copy(n, dx, fy).start()

        @pl.when(side != yl)
        def _():
            for n, (dx, fy) in enumerate(plane):
                if fy == 1:
                    p_copy(n, dx, fy).start()

    for dy in (0, 1, 3, 2):
        d_c(0, dy).wait_recv()
    terms(0)
    for dy in (0, 1, 3, 2):
        d_z(dy).wait_recv()
        d_c(1, dy).start()
    for dy in (0, 1, 3, 2):
        d_c(1, dy).wait_recv()
    terms(1)

    def g_copy(n, dza, fc):
        return remote(
            gsend.at[(za + dza) % 4, (c + fc) % 2], grecv.at[za, c], S_G + n, far(dza, fc)
        )

    def g_arrival(n, dza, fc):
        return remote(
            gsend.at[0, 0], grecv.at[(za + 4 - dza) % 4, (c + fc) % 2], S_G + n, sibling
        )

    for n, (dx, fy) in enumerate(plane):
        h_arrival(n, dx, fy).wait_recv()
    for j in range(2):
        out = nn_dot(hall[0].reshape(512, 512), dall[j, 0].reshape(512, 256))
        out = out + nn_dot(hall[1].reshape(512, 512), dall[j, 1].reshape(512, 256))
        out = (out * (1.0 / 64.0)).astype(BF16)
        for k in range(4):
            gsend[k, j] = out[k * 128 : (k + 1) * 128, :]
    for n, (dza, fc) in enumerate(depth):
        g_copy(n, dza, fc).start()

    for n, (dx, fy) in enumerate(plane):
        p_arrival(n, dx, fy).wait_recv()
    acc = psend[yl, x].astype(F32)
    for n, (dx, fy) in enumerate(plane):
        sx, sy = plane_src(dx, fy)
        acc = acc + precv[sy, sx].astype(F32)
    rsum[...] = acc.astype(BF16).reshape(4, 128, 128)

    def q_copy(ys):
        return remote(
            rsum.at[ys], qrecv.at[yh % 2, c], S_Q + ys, hid_source(ys), S_Q + 2 * (yh % 2) + c
        )

    for ys in range(4):

        @pl.when(jnp.logical_not(hid_source_is_me(ys)))
        def _():
            q_copy(ys).start()

        @pl.when(hid_source_is_me(ys))
        def _():
            own = pltpu.make_async_copy(rsum.at[ys], qrecv.at[yh % 2, c], lsem)
            own.start()
            own.wait()

    for n, (dza, fc) in enumerate(depth):
        g_arrival(n, dza, fc).wait_recv()
    grecv[za, c] = gsend[za, c]
    for h in range(2):
        acc = grecv[0, h].astype(F32)
        for k in range(1, 4):
            acc = acc + grecv[k, h].astype(F32)
        wgrad_ref[h * 128 : (h + 1) * 128, :] = acc.astype(BF16)

    for i in range(2):
        for h in range(2):

            @pl.when(jnp.logical_not(hid_target_is_me(i, h)))
            def _():
                remote(
                    rsum.at[0], qrecv.at[i, h], S_Q + 2 * i + h, sibling
                ).wait_recv()

    grad = jnp.concatenate([qrecv[0, 0], qrecv[0, 1], qrecv[1, 0], qrecv[1, 1]], axis=1)
    grad = grad.astype(F32) * gain
    sums[1, 0] = row_of(jnp.sum(grad * hid, axis=1, keepdims=True))
    sum_sibling(1, S_MEAN).start()
    sum_sibling(1, S_MEAN).wait_recv()
    sums[1, 1] = sums[1, 0] + sums_in[1, 0]
    for n, (dx, fy) in enumerate(plane):
        sum_plane(1, S_MEAN, n, dx, fy).start()
    for n, (dx, fy) in enumerate(plane):
        sum_plane(1, S_MEAN, n, dx, fy).wait_recv()
    dot = sums[1, 1]
    for n in range(7):
        dot = dot + sums_in[1, 1 + n]
    factor = column_of(dot) * (1.0 / 8192.0) / mean_square
    for k in range(4):
        part = slice(k * 128, (k + 1) * 128)
        igrad_ref[:, part] = (grad[:, part] - hid[:, part] * factor).astype(BF16)

    for i in range(2):
        for h in range(2):

            @pl.when(jnp.logical_not(hid_target_is_me(i, h)))
            def _():
                hid_copy(i, h).wait_send()

    for ys in range(4):

        @pl.when(jnp.logical_not(hid_source_is_me(ys)))
        def _():
            q_copy(ys).wait_send()

    for which, base in ((0, S_SQ), (1, S_MEAN)):
        sum_sibling(which, base).wait_send()
        for n, (dx, fy) in enumerate(plane):
            sum_plane(which, base, n, dx, fy).wait_send()
    gram_copy.wait_send()
    for n, (dza, fc) in enumerate(depth):
        w_copy(n, dza, fc).wait_send()
        g_copy(n, dza, fc).wait_send()
    for n, (dx, fy) in enumerate(plane):
        h_copy(n, dx, fy).wait_send()
        p_copy(n, dx, fy).wait_send()
    for dy in range(4):
        if dy:
            d_y(dy).wait_send()
        d_z(dy).wait_send()
        d_c(0, dy).wait_send()
        d_c(1, dy).wait_send()


def shards(hidden, gain, proj_weight, b_c, ssm_x, dy, log_decay):
    vmem = pl.BlockSpec(memory_space=pltpu.VMEM)
    return pl.pallas_call(
        kernel,
        out_shape=(
            jax.ShapeDtypeStruct(hidden.shape, BF16),
            jax.ShapeDtypeStruct(proj_weight.shape, BF16),
        ),
        in_specs=[vmem] * 7,
        out_specs=(vmem, vmem),
        scratch_shapes=[
            pltpu.VMEM((4, 128, 128), BF16),
            pltpu.VMEM((2, 4, 128, 512), BF16),
            pltpu.VMEM((2, 4, 128, 256), BF16),
            pltpu.VMEM((2, 2, 8, 128), F32),
            pltpu.VMEM((2, 8, 8, 128), F32),
            pltpu.VMEM((2, 128, 128), F32),
            pltpu.VMEM((2, 2, 4, 128, 256), BF16),
            pltpu.VMEM((2, 4, 512, 128), BF16),
            pltpu.VMEM((2, 4, 512, 128), BF16),
            pltpu.VMEM((4, 128, 128), BF16),
            pltpu.VMEM((2, 2, 128, 128), BF16),
            pltpu.VMEM((4, 2, 128, 256), BF16),
            pltpu.VMEM((4, 2, 128, 256), BF16),
            pltpu.SemaphoreType.DMA((N_SLOTS,)),
            pltpu.SemaphoreType.DMA((N_SLOTS,)),
            pltpu.SemaphoreType.DMA,
        ],
        compiler_params=pltpu.CompilerParams(
            collective_id=0, has_side_effects=True, vmem_limit_bytes=40 * 1024 * 1024
        ),
        name="projection_backward",
    )(hidden, gain.reshape(1, -1), proj_weight, b_c, ssm_x, dy, log_decay)


def solution(mesh):
    return jax.shard_map(
        shards,
        mesh=mesh,
        in_specs=(
            P("dp", "tensor"),
            P("tensor"),
            P("dp", "tensor"),
            P("dp", "tensor"),
            P("dp", "tensor"),
            P("dp", "tensor"),
            P("dp", "tensor"),
        ),
        out_specs=(P("dp", "tensor"), P("dp", "tensor")),
        check_vma=False,
    )
```

time: 538 us -> 70.4 us (0.13)
  waiting for transfers between devices: 469 us -> 0 us
  Pallas kernels: 0 us -> 62.9 us
  blocking collectives: 21.3 us -> 0 us
  between operations: 13.9 us -> 0.66 us
  matrix products: 12.5 us -> 0 us
  starting transfers between devices: 8.94 us -> 0 us
  other arithmetic: 5.66 us -> 0 us
    reduce_scatter x1 -> x0, waiting for transfers between devices: 230 us -> none  [shards(): lax.psum_scatter((lax.dot_general(normed, dproj, (((0,), (0,)), ((), ()))...]
    psum x1 -> x0, waiting for transfers between devices: 130 us -> none  [shards(): lax.psum(partial_grad.astype(jnp.bfloat16), 'tensor').astype(jnp.float32)]
    all_gather x2 -> x0, waiting for transfers between devices: 106 us -> none  [the longest x1 93.1 us: shards(): lax.all_gather(proj_weight, 'dp', axis=0, tiled=True)]
    pallas_call x0 -> x1, Pallas kernels: none -> 62.9 us  [shards(): pl.pallas_call(kernel, out_shape=(jax.ShapeDtypeStruct(hidden.shape, BF16...]
    all_gather x1 -> x0, blocking collectives: 21.3 us -> none  [shards(): lax.all_gather(gain, 'tensor', axis=0, tiled=True)]
    dot_general x5 -> x0, matrix products: 12.5 us -> none  [the longest x1 5.07 us: shards(): lax.dot_general(dproj, lax.all_gather(proj_weight, 'dp', axis=0, tiled=Tr...]
    ppermute x1 -> x0, starting transfers between devices: 8.79 us -> none  [swapped(): return lax.ppermute(value, axis, pairs)]
  transfers between devices with their start and end apart: 5 -> 0, of which waited for: 5 -> 0; matrix products, arithmetic and copies ran while one was open for 4% -> 0% of each run, Pallas kernels for 0% -> 0%
where the time goes in v1:
time: 70.4 us; the launch traced here: 70.1 us
  Pallas kernels  62.9 us (89%)
  local copies, waits for them, and re-layouts  6.53 us (9%)
    pallas_call x1, Pallas kernels, shards(): pl.pallas_call(kernel, out_shape=(jax.ShapeDtypeStruct(hidden.shape, BF16...  62.9 us
    unnamed x13, local copies, waits for them, and re-layouts  5.81 us

profile of v1, /device:TPU:1, one launch (start us, length us, event | category | flops | bytes accessed | tf_op | source)
XLA Modules:
  0.0 70.1 jit_solution(17757934421697117331)
XLA Ops:
  0.6 0.0 copy-start.4
  0.6 0.7 %reshape.7.gain_ref = bf16[1,512]{1,0:T(2,128)(2,1)S(1)} reshape(bf16[512]{0:T(512)(128)(2,1)} %param.8) | data formatting | bytes 2048 | tf_op jit(solution)/shard_map/reshape | solution.py:505
  1.4 0.8 %copy.9.ld_ref = f32[128,16]{1,0:T(8,128)S(1)} copy(f32[128,16]{0,1:T(8,128)} %param.13) | data formatting | bytes 16384 | tf_op args[6]
  2.1 0.0 copy-done.4
  2.2 0.0 copy-start
  2.2 0.9 %copy-done = bf16[128,1024]{1,0:T(8,128)(2,1)S(1)} copy-done((bf16[128,1024]{1,0:T(8,128)(2,1)S(1)}, bf16[128,1024]{1,0:T(8,128)(2,1)}, u32[]{:S(2)}) %copy-start) | copy-done | bytes 262168
  3.1 0.0 copy-start.1
  3.1 0.9 %copy-done.1 = bf16[128,1024]{1,0:T(8,128)(2,1)S(1)} copy-done((bf16[128,1024]{1,0:T(8,128)(2,1)S(1)}, bf16[128,1024]{1,0:T(8,128)(2,1)}, u32[]{:S(2)}) %copy-start.1) | copy-done | bytes 262168
  4.1 0.0 copy-start.2
  4.1 0.9 %copy-done.2 = bf16[128,512]{1,0:T(8,128)(2,1)S(1)} copy-done((bf16[128,512]{1,0:T(8,128)(2,1)S(1)}, bf16[128,512]{1,0:T(8,128)(2,1)}, u32[]{:S(2)}) %copy-start.2) | copy-done | bytes 131096
  5.0 0.0 copy-start.3
  5.0 0.9 %copy-done.3 = bf16[256,256]{1,0:T(8,128)(2,1)S(1)} copy-done((bf16[256,256]{1,0:T(8,128)(2,1)S(1)}, bf16[256,256]{1,0:T(8,128)(2,1)}, u32[]{:S(2)}) %copy-start.3) | copy-done | bytes 131096
  5.9 62.9 %projection_backward.1 = (bf16[128,512]{1,0:T(8,128)(2,1)S(1)}, bf16[256,256]{1,0:T(8,128)(2,1)S(1)}) custom-call(bf16[128,512]{1,0:T(8,128)(2,1)S(1)} %copy-done.2, bf16[1,512]{1,0:T(2,128)(2,1)S(1)} %reshape.7.gain_ref, bf16[256,256]{1,0:T(8,128)(2,1)S(1)} %copy-done.3, bf16[128,256]{1,0:T(8,128)(2,1)S(1)} %copy-done.4, bf16[128,1024]{1,0:T(8,128)(2,1)S(1)} %copy-done, ...), custom_call_target="tpu_custom_call" | custom-call | tf_op jit(solution)/shard_map/projection_backward/pallas_call | solution.py:475
  68.8 0.7 copy.12
  69.5 0.7 copy.13
Async XLA Ops:
  0.6 1.5 %copy-start.4 = (bf16[128,256]{1,0:T(8,128)(2,1)S(1)}, bf16[128,256]{1,0:T(8,128)(2,1)}, u32[]{:S(2)}) copy-start(bf16[128,256]{1,0:T(8,128)(2,1)} %bc_ref.1) | copy-start | bytes 196612
  2.2 1.0 %copy-start = (bf16[128,1024]{1,0:T(8,128)(2,1)S(1)}, bf16[128,1024]{1,0:T(8,128)(2,1)}, u32[]{:S(2)}) copy-start(bf16[128,1024]{1,0:T(8,128)(2,1)} %x_ref.1) | copy-start | bytes 786436
  3.1 0.9 %copy-start.1 = (bf16[128,1024]{1,0:T(8,128)(2,1)S(1)}, bf16[128,1024]{1,0:T(8,128)(2,1)}, u32[]{:S(2)}) copy-start(bf16[128,1024]{1,0:T(8,128)(2,1)} %dy_ref.1) | copy-start | bytes 786436
  4.1 0.9 %copy-start.2 = (bf16[128,512]{1,0:T(8,128)(2,1)S(1)}, bf16[128,512]{1,0:T(8,128)(2,1)}, u32[]{:S(2)}) copy-start(bf16[128,512]{1,0:T(8,128)(2,1)} %hid_ref.1) | copy-start | bytes 393220
  5.0 0.9 %copy-start.3 = (bf16[256,256]{1,0:T(8,128)(2,1)S(1)}, bf16[256,256]{1,0:T(8,128)(2,1)}, u32[]{:S(2)}) copy-start(bf16[256,256]{1,0:T(8,128)(2,1)} %w_ref.1) | copy-start | bytes 393220

commit v2 on v1

v2 whole, which is shorter than its diff:
```python
import jax
import jax.numpy as jnp
from jax import lax
from jax.experimental import pallas as pl
from jax.experimental.pallas import tpu as pltpu
from jax.sharding import PartitionSpec as P

MHEAD = 64
EPSILON = 1e-05
MESH = pl.DeviceIdType.MESH
F32 = jnp.float32
BF16 = jnp.bfloat16
HIGHEST = lax.Precision.HIGHEST


def device(za, zb, yh, x, yl, c):
    return {"dp": (za * 2 + zb) * 4 + yh, "tensor": x * 4 + yl * 2 + c}


def nt_dot(a, b, precision=None):
    return lax.dot_general(
        a, b, (((1,), (1,)), ((), ())), preferred_element_type=F32, precision=precision
    )


def nn_dot(a, b, precision=None):
    return lax.dot_general(
        a, b, (((1,), (0,)), ((), ())), preferred_element_type=F32, precision=precision
    )


class Slots:
    def __init__(self):
        self.count = 0

    def take(self, n):
        first = self.count
        self.count += n
        return first


SLOTS = Slots()
S_HID = SLOTS.take(4)
S_HAG = SLOTS.take(14)
S_W = SLOTS.take(7)
S_SQ = SLOTS.take(8)
S_INV = SLOTS.take(8)
S_GRAM = SLOTS.take(1)
S_DY = SLOTS.take(4)
S_DZ = SLOTS.take(4)
S_DC = SLOTS.take(8)
S_P = SLOTS.take(14)
S_Q = SLOTS.take(4)
S_G = SLOTS.take(7)
S_DOT = SLOTS.take(8)
S_MEAN = SLOTS.take(15)
N_SLOTS = SLOTS.count


def kernel(
    hid_hbm,
    gain_hbm,
    w_hbm,
    bc_hbm,
    x_hbm,
    dy_hbm,
    ld_hbm,
    igrad_hbm,
    wgrad_hbm,
    igrad_ref,
    wgrad_ref,
    hid_ref,
    gain_ref,
    w_ref,
    bc_ref,
    x_ref,
    dy_ref,
    ld_ref,
    ht,
    hall,
    hscaled,
    wall,
    sums,
    sums_in,
    inv,
    dots,
    dots_in,
    gram,
    dall,
    psend,
    precv,
    rsum,
    qrecv,
    gsend,
    grecv,
    grelay,
    ssem,
    rsem,
    lsem,
    isem,
):
    loads = [
        pltpu.make_async_copy(src, dst, isem.at[n])
        for n, (src, dst) in enumerate(
            (
                (ld_hbm, ld_ref),
                (x_hbm, x_ref),
                (dy_hbm, dy_ref),
                (hid_hbm, hid_ref),
                (gain_hbm, gain_ref),
                (w_hbm, w_ref),
                (bc_hbm, bc_ref),
            )
        )
    ]
    for load in loads:
        load.start()

    dp = lax.axis_index("dp")
    ten = lax.axis_index("tensor")
    z, yh = dp // 4, dp % 4
    za, zb = z // 2, z % 2
    x, yl, c = ten // 4, (ten // 2) % 2, ten % 2

    def remote(src, dst, slot, dev, rslot=None):
        rslot = slot if rslot is None else rslot
        return pltpu.make_async_remote_copy(
            src_ref=src,
            dst_ref=dst,
            send_sem=ssem.at[slot],
            recv_sem=rsem.at[rslot],
            device_id=device(*dev),
            device_id_type=MESH,
        )

    sibling = (za, zb, yh, x, yl, 1 - c)
    plane = [(1, 0), (3, 0), (2, 0), (0, 1), (1, 1), (3, 1), (2, 1)]
    column = [(0, 1), (0, 3), (0, 2), (1, 0), (1, 1), (1, 3), (1, 2)]
    depth = [(dza, fc) for dza in (1, 3) for fc in range(2)] + [(0, 1)]
    tensor = [(0, 0, 1)] + [(dx, fy, fc) for fc in range(2) for dx, fy in plane]

    def plane_dev(dx, fy):
        return (za, zb, yh, (x + dx) % 4, (yl + fy) % 2, c)

    def plane_src(dx, fy):
        return (x + 4 - dx) % 4, (yl + fy) % 2

    def tensor_dev(dx, fy, fc):
        return (za, zb, yh, (x + dx) % 4, (yl + fy) % 2, (c + fc) % 2)

    def column_dev(k, dy):
        return (za, (zb + k) % 2, (yh + dy) % 4, x, yl, c)

    def far(dza, fc):
        return ((za + dza) % 4, zb, yh, x, yl, (c + fc) % 2)

    def seq(side, y):
        return (y % 2, side, y // 2)

    def hid_target(i, h):
        return (za, yl, 2 * c + i, x, yh % 2, h)

    def hid_target_is_me(i, h):
        return (yl == zb) & (yh == 2 * c + i) & (yl == yh % 2) & (c == h)

    def hid_source(side, u):
        return (za, side, yl + 2 * u, x, zb, yh // 2)

    def hid_source_is_me(side, u):
        return (side == zb) & (yl + 2 * u == yh) & (yl == zb) & (c == yh // 2)

    barrier = pltpu.get_barrier_semaphore()

    def greet(dev):
        pl.semaphore_signal(barrier, inc=1, device_id=device(*dev), device_id_type=MESH)

    for dx, fy, fc in tensor:
        greet(tensor_dev(dx, fy, fc))
    for k, dy in column:
        greet(column_dev(k, dy))
    for dza, fc in depth[:-1]:
        greet(far(dza, fc))
    met = 15 + 7 + 4
    for i in range(2):
        for h in range(2):

            @pl.when(jnp.logical_not(hid_target_is_me(i, h)))
            def _():
                greet(hid_target(i, h))

    for side in range(2):
        for u in range(2):

            @pl.when(jnp.logical_not(hid_source_is_me(side, u)))
            def _():
                greet(hid_source(side, u))

    own_hop = jnp.where((yl == zb) & (yl == yh % 2) & (c == yh // 2), 1, 0)

    for load in loads[:3]:
        load.wait()
    rows = lax.broadcasted_iota(jnp.int32, (128, 128), 0)
    cols = lax.broadcasted_iota(jnp.int32, (128, 128), 1)
    causal = rows >= cols
    heads = ld_ref.shape[0]
    padded = jnp.concatenate([ld_ref[...], jnp.zeros((128 - heads, 128), F32)], axis=0)
    running_t = nt_dot(padded, causal.astype(F32), HIGHEST)
    running = running_t.T
    low = cols < MHEAD
    total = jnp.zeros((128, 128), F32)
    for p in range(heads // 2):
        xp = x_ref[:, p * 128 : (p + 1) * 128]
        zero = jnp.zeros_like(xp)
        both = jnp.concatenate([jnp.where(low, xp, zero), jnp.where(low, zero, xp)], axis=0)
        inner = nt_dot(dy_ref[:, p * 128 : (p + 1) * 128], both)
        for k in range(2):
            h = 2 * p + k
            gap = running[:, h : h + 1] - running_t[h : h + 1, :]
            decay = jnp.exp(jnp.where(causal, gap, -1e30))
            total = total + inner[:, k * 128 : (k + 1) * 128] * decay
    gram[0] = total

    for load in loads[3:]:
        load.wait()
    hid = hid_ref[...].astype(F32)
    gain = gain_ref[...].astype(F32).reshape(1, -1)
    scaled = hid * gain
    for k in range(4):
        ht[k] = scaled[:, k * 128 : (k + 1) * 128].T.astype(BF16)

    def row_of(column):
        return jnp.broadcast_to(column, (128, 128)).T[0:8, :]

    def column_of(row):
        return jnp.broadcast_to(row[0:1, :], (128, 128)).T

    sums[0] = row_of(jnp.sum(hid * hid, axis=1, keepdims=True))
    wall[c, za] = w_ref[pl.ds(pl.multiple_of(c * 128, 128), 128), :]

    pl.semaphore_wait(barrier, met + 8 - 2 * own_hop)

    gram_copy = remote(gram.at[0], gram.at[1], S_GRAM, sibling)
    gram_copy.start()

    sq_sibling = remote(sums.at[0], sums_in.at[0, 0], S_SQ, sibling)
    sq_sibling.start()

    def sq_copy(n):
        return remote(sums.at[1], sums_in.at[0, 1 + n], S_SQ + 1 + n, plane_dev(*plane[n]))

    def mean_copy(n):
        return remote(sums.at[2], sums_in.at[1, n], S_MEAN + n, tensor_dev(*tensor[n]))

    def hid_copy(i, h):
        lane = (2 * zb + yh // 2) * 128
        return remote(
            ht.at[2 * i + h],
            hall.at[yh % 2, x, :, pl.ds(pl.multiple_of(lane, 128), 128)],
            S_HID + 2 * i + h,
            hid_target(i, h),
            S_HID + 2 * zb + yh // 2,
        )

    def hid_arrival(side, u):
        lane = (2 * side + u) * 128
        return remote(
            ht.at[0],
            hall.at[yl, x, :, pl.ds(pl.multiple_of(lane, 128), 128)],
            S_HID + 2 * side + u,
            sibling,
        )

    for i in range(2):
        for h in range(2):

            @pl.when(jnp.logical_not(hid_target_is_me(i, h)))
            def _():
                hid_copy(i, h).start()

            @pl.when(hid_target_is_me(i, h))
            def _():
                lane = (2 * zb + yh // 2) * 128
                own = pltpu.make_async_copy(
                    ht.at[2 * i + h],
                    hall.at[yl, x, :, pl.ds(pl.multiple_of(lane, 128), 128)],
                    lsem,
                )
                own.start()
                own.wait()

    def w_copy(n):
        dza, fc = depth[n]
        core = (c + fc) % 2
        return remote(
            w_ref.at[pl.ds(pl.multiple_of(core * 128, 128), 128), :],
            wall.at[c, za],
            S_W + n,
            far(dza, fc),
        )

    def w_arrival(n):
        dza, fc = depth[n]
        return remote(
            w_ref.at[0:128, :], wall.at[(c + fc) % 2, (za + 4 - dza) % 4], S_W + n, sibling
        )

    for n in range(5):
        w_copy(n).start()

    def w_on(j):
        block = wall.at[j, (za + (1, 3)[j] + 2) % 4]
        return remote(block, block, S_W + 5 + j, far((1, 3)[j], 0))

    def w_on_arrival(j):
        block = wall.at[j, (za + 2) % 4]
        return remote(block, block, S_W + 5 + j, sibling)

    sq_sibling.wait_recv()
    sums[1] = sums[0] + sums_in[0, 0]
    for n in range(7):
        sq_copy(n).start()

    gram_copy.wait_recv()
    total = gram[0] + gram[1]
    bc = bc_ref[...].astype(F32)
    grad_b = nn_dot(total.T, bc[:, 128:], HIGHEST)
    grad_c = nn_dot(total, bc[:, :128], HIGHEST)
    dall[(c,) + seq(zb, yh)] = jnp.concatenate([grad_b, grad_c], axis=1).astype(BF16)

    def d_y(dy):
        block = dall.at[(c,) + seq(zb, yh)]
        return remote(block, block, S_DY + dy, column_dev(0, dy))

    def d_y_arrival(dy):
        block = dall.at[(c,) + seq(zb, (yh + 4 - dy) % 4)]
        return remote(block, block, S_DY + dy, sibling)

    def d_z(dy):
        if dy == 2:
            block = dall.at[(c,) + seq(1 - zb, yh)]
            return remote(block, block, S_DZ + dy, column_dev(0, 2))
        block = dall.at[(c,) + seq(zb, (yh + 4 - dy) % 4)]
        return remote(block, block, S_DZ + dy, column_dev(1, 0))

    def d_z_arrival(dy):
        block = dall.at[(c,) + seq(1 - zb, (yh + 4 - dy) % 4)]
        return remote(block, block, S_DZ + dy, sibling)

    def d_c(k, dy):
        block = dall.at[(c,) + seq((zb + k) % 2, (yh + 4 - dy) % 4)]
        return remote(block, block, S_DC + 4 * k + dy, sibling)

    def d_c_arrival(k, dy):
        block = dall.at[(1 - c,) + seq((zb + k) % 2, (yh + 4 - dy) % 4)]
        return remote(block, block, S_DC + 4 * k + dy, sibling)

    for dy in (1, 3):
        d_y(dy).start()
    d_z(0).start()
    d_c(0, 0).start()

    square = sums[1]
    for n in range(7):
        sq_copy(n).wait_recv()
        square = square + sums_in[0, 1 + n]
    mean_square = square * (1.0 / 8192.0) + EPSILON
    inv_root = lax.rsqrt(mean_square)
    inv[seq(zb, yh)] = inv_root

    def inv_copy(n):
        block = inv.at[seq(zb, yh)]
        return remote(block, block, S_INV + n, column_dev(*column[n]))

    def inv_arrival(n):
        k, dy = column[n]
        block = inv.at[seq((zb + k) % 2, (yh + 4 - dy) % 4)]
        return remote(block, block, S_INV + n, sibling)

    for n in range(7):
        inv_copy(n).start()

    def h_block(k, sy, sx):
        lane = ((zb + k) % 2) * 256
        return hall.at[sy, sx, :, pl.ds(pl.multiple_of(lane, 128), 256)]

    def h_copy(k, n):
        dx, fy = plane[n]
        block = h_block(k, (yl + fy) % 2 if dx else yl, x)
        dev = (za, zb, yh, (x + dx) % 4, yl if dx else 1 - yl, c)
        return remote(block, block, S_HAG + 7 * k + n, dev)

    def h_arrival(k, n):
        sx, sy = plane_src(*plane[n])
        block = h_block(k, sy, sx)
        return remote(block, block, S_HAG + 7 * k + n, sibling)

    def hid_on(k):
        side = (zb + k) % 2
        for u in range(2):

            @pl.when(jnp.logical_not(hid_source_is_me(side, u)))
            def _():
                hid_arrival(side, u).wait_recv()

        for n in (3, 0, 1, 2):
            h_copy(k, n).start()

    def hid_across(k):
        h_arrival(k, 3).wait_recv()
        for n in range(4, 7):
            h_copy(k, n).start()

    hid_on(0)
    hid_on(1)
    d_y(2).start()

    def d_on(dy):
        d_y_arrival(dy).wait_recv()
        if dy != 2:
            d_z(dy).start()
        d_c(0, dy).start()

    d_on(1)
    d_on(3)
    hid_across(0)
    d_z_arrival(0).wait_recv()
    d_z(2).start()
    d_c(1, 0).start()
    for n in range(4):
        w_arrival(n).wait_recv()
    for j in range(2):
        w_on(j).start()
    hid_across(1)
    d_on(2)

    for dy in (0, 1, 3, 2):
        d_c_arrival(0, dy).wait_recv()

    def p_copy(k, n):
        dx, fy = plane[n]
        side = (zb + k) % 2
        return remote(
            psend.at[side, (yl + fy) % 2, (x + dx) % 4],
            precv.at[side, yl, x],
            S_P + 7 * k + n,
            plane_dev(dx, fy),
        )

    def p_arrival(k, n):
        sx, sy = plane_src(*plane[n])
        block = precv.at[(zb + k) % 2, sy, sx]
        return remote(block, block, S_P + 7 * k + n, sibling)

    def terms(k, dza):
        side, tx = (zb + k) % 2, (za + dza) % 4
        for py in range(2):
            out = nt_dot(dall[0, py, side].reshape(256, 256), wall[0, tx])
            out = out + nt_dot(dall[1, py, side].reshape(256, 256), wall[1, tx])
            psend[side, py, tx] = out.astype(BF16)

    def p_start(k, dza):
        for n, (dx, fy) in enumerate(plane):

            @pl.when((x + dx) % 4 == (za + dza) % 4)
            def _():
                p_copy(k, n).start()

    w_arrival(4).wait_recv()
    terms(0, 0)
    p_start(0, 0)
    terms(0, 1)
    p_start(0, 1)
    terms(0, 3)
    p_start(0, 3)
    for j in range(2):
        w_on_arrival(j).wait_recv()
    terms(0, 2)
    p_start(0, 2)
    for dy in (1, 3, 2):
        d_z_arrival(dy).wait_recv()
        d_c(1, dy).start()
    for dy in (0, 1, 3, 2):
        d_c_arrival(1, dy).wait_recv()
    for dza in range(4):
        terms(1, dza)

    def g_copy(d, j):
        dza = (1, 3)[d]
        dev = ((za + dza) % 4, zb, yh, x, yl, j)
        return remote(
            gsend.at[(za + dza) % 4, j], grecv.at[za, c], S_G + 2 * d + j, dev, S_G + 2 * d + c
        )

    def g_arrival(d, h):
        block = grecv.at[(za + (3, 1)[d]) % 4, h]
        return remote(block, block, S_G + 2 * d + h, sibling)

    def g_sibling():
        return remote(gsend.at[za, 1 - c], grecv.at[za, c], S_G + 4, sibling)

    def g_relay(j):
        return remote(
            gsend.at[(za + 2) % 4, j], grelay.at[j], S_G + 5 + j, far((1, 3)[j], 0)
        )

    for n in range(7):
        inv_arrival(n).wait_recv()
    inv_rows = [
        jnp.concatenate([inv[sy, side, u][0:1, :] for side in range(2) for u in range(2)], axis=1)
        for sy in range(2)
    ]
    inv_rows = [inv_rows[sy] * (1.0 / 64.0) for sy in range(2)]
    own_inv = jnp.where(yl == 0, inv_rows[0], inv_rows[1])
    other_inv = jnp.where(yl == 0, inv_rows[1], inv_rows[0])

    def scale(dx, fy):
        sx, sy = plane_src(dx, fy)
        row = other_inv if fy else own_inv
        hscaled[sy, sx] = (hall[sy, sx].astype(F32) * row).astype(BF16)

    scale(0, 0)
    scale(0, 1)
    for n in (0, 1, 2, 4, 5, 6):
        h_arrival(0, n).wait_recv()
        h_arrival(1, n).wait_recv()
        scale(*plane[n])
    eye = (rows == cols).astype(F32)
    for py in range(2):
        for side in range(2):
            for u in range(2):
                part = slice(u * 128, (u + 1) * 128)
                lane = (2 * side + u) * 128
                prod = jnp.zeros((128, 128), F32)
                for f in range(4):
                    prod = prod + nn_dot(
                        psend[side, py, f, part, :], hall[py, f, :, lane : lane + 128]
                    )
                row = jnp.sum(prod * eye, axis=0, keepdims=True)
                dots[py, side, u] = jnp.broadcast_to(row, (8, 128))

    def dot_copy(n):
        k, dy = column[n]
        block = dots.at[seq((zb + k) % 2, (yh + dy) % 4)]
        return remote(block, dots_in.at[n], S_DOT + n, column_dev(k, dy))

    for n in range(7):
        dot_copy(n).start()
    for n in range(7):
        p_copy(1, n).start()

    for j in range(2):
        out = nn_dot(hscaled[0].reshape(512, 512), dall[j, 0].reshape(512, 256))
        out = out + nn_dot(hscaled[1].reshape(512, 512), dall[j, 1].reshape(512, 256))
        out = out.astype(BF16)
        for k in range(4):
            gsend[k, j] = out[k * 128 : (k + 1) * 128, :]
    for j in range(2):
        g_relay(j).start()
    g_copy(0, 1).start()
    g_copy(1, 0).start()
    g_sibling().start()

    def q_copy(k, u):
        side = (zb + k) % 2
        return remote(
            rsum.at[side, u],
            qrecv.at[yh % 2, c],
            S_Q + 2 * k + u,
            hid_source(side, u),
            S_Q + 2 * (yh % 2) + c,
        )

    def owners(k):
        side = (zb + k) % 2
        for n in range(7):
            p_arrival(k, n).wait_recv()
        acc = psend[side, yl, x].astype(F32)
        for n in range(7):
            sx, sy = plane_src(*plane[n])
            acc = acc + precv[side, sy, sx].astype(F32)
        rsum[side] = acc.astype(BF16).reshape(2, 128, 128)
        for u in range(2):

            @pl.when(jnp.logical_not(hid_source_is_me(side, u)))
            def _():
                q_copy(k, u).start()

            @pl.when(hid_source_is_me(side, u))
            def _():
                own = pltpu.make_async_copy(rsum.at[side, u], qrecv.at[yh % 2, c], lsem)
                own.start()
                own.wait()

    owners(0)
    for j in range(2):
        g_relay(j).wait_recv()
        to = (za + (1, 3)[j]) % 4
        gsend[to, j] = (gsend[to, j].astype(F32) + grelay[j].astype(F32)).astype(BF16)
        g_copy(j, j).start()

    for n in range(7):
        dot_copy(n).wait_recv()
    value = dots[seq(zb, yh)]
    for n in range(7):
        value = value + dots_in[n]
    sums[2] = value
    for n in range(15):
        mean_copy(n).start()
    owners(1)

    g_sibling().wait_recv()
    for h in range(2):
        for d in range(2):
            g_arrival(d, h).wait_recv()
    grecv[za, c] = gsend[za, c]
    for h in range(2):
        acc = grecv[za, h].astype(F32)
        for d in range(2):
            acc = acc + grecv[(za + (3, 1)[d]) % 4, h].astype(F32)
        wgrad_ref[h * 128 : (h + 1) * 128, :] = acc.astype(BF16)

    wgrad_out = pltpu.make_async_copy(wgrad_ref, wgrad_hbm, isem.at[7])
    wgrad_out.start()
    dot = sums[2]
    for n in range(15):
        mean_copy(n).wait_recv()
        dot = dot + sums_in[1, n]
    factor = column_of(dot * (1.0 / 8192.0) / mean_square)
    inv_column = column_of(inv_root)
    for i in range(2):
        for h in range(2):

            @pl.when(jnp.logical_not(hid_target_is_me(i, h)))
            def _():
                remote(rsum.at[0, 0], qrecv.at[i, h], S_Q + 2 * i + h, sibling).wait_recv()

    for i in range(2):
        for h in range(2):
            k = 2 * i + h
            part = slice(k * 128, (k + 1) * 128)
            grad = qrecv[i, h].astype(F32) * gain[:, part]
            igrad_ref[:, part] = ((grad - hid[:, part] * factor) * inv_column).astype(BF16)

    igrad_out = pltpu.make_async_copy(igrad_ref, igrad_hbm, isem.at[8])
    igrad_out.start()

    for i in range(2):
        for h in range(2):

            @pl.when(jnp.logical_not(hid_target_is_me(i, h)))
            def _():
                hid_copy(i, h).wait_send()

    for k in range(2):
        for u in range(2):

            @pl.when(jnp.logical_not(hid_source_is_me((zb + k) % 2, u)))
            def _():
                q_copy(k, u).wait_send()

    sq_sibling.wait_send()
    for n in range(7):
        sq_copy(n).wait_send()
    for n in range(15):
        mean_copy(n).wait_send()
    gram_copy.wait_send()
    for n in range(5):
        w_copy(n).wait_send()
    g_sibling().wait_send()
    for j in range(2):
        w_on(j).wait_send()
        g_relay(j).wait_send()
        for d in range(2):
            g_copy(d, j).wait_send()
    for n in range(7):
        h_copy(0, n).wait_send()
        h_copy(1, n).wait_send()
        p_copy(0, n).wait_send()
        p_copy(1, n).wait_send()
        inv_copy(n).wait_send()
        dot_copy(n).wait_send()
    for dy in range(4):
        if dy:
            d_y(dy).wait_send()
        d_z(dy).wait_send()
        d_c(0, dy).wait_send()
        d_c(1, dy).wait_send()
    wgrad_out.wait()
    igrad_out.wait()


def hand_over(igrad_ref, wgrad_ref, igrad_out, wgrad_out, igrad, wgrad, sem):
    ins = [
        pltpu.make_async_copy(igrad_ref, igrad, sem.at[0]),
        pltpu.make_async_copy(wgrad_ref, wgrad, sem.at[1]),
    ]
    outs = [
        pltpu.make_async_copy(igrad, igrad_out, sem.at[2]),
        pltpu.make_async_copy(wgrad, wgrad_out, sem.at[3]),
    ]
    for copy in ins:
        copy.start()
    for first, second in zip(ins, outs):
        first.wait()
        second.start()
    for copy in outs:
        copy.wait()


def shards(hidden, gain, proj_weight, b_c, ssm_x, dy, log_decay):
    hbm = pl.BlockSpec(memory_space=pl.ANY)
    grads = pl.pallas_call(
        kernel,
        out_shape=(
            jax.ShapeDtypeStruct(hidden.shape, BF16),
            jax.ShapeDtypeStruct(proj_weight.shape, BF16),
        ),
        in_specs=[hbm] * 7,
        out_specs=(hbm, hbm),
        scratch_shapes=[
            pltpu.VMEM(hidden.shape, BF16),
            pltpu.VMEM(proj_weight.shape, BF16),
            pltpu.VMEM(hidden.shape, BF16),
            pltpu.VMEM(gain.shape, BF16),
            pltpu.VMEM(proj_weight.shape, BF16),
            pltpu.VMEM(b_c.shape, BF16),
            pltpu.VMEM(ssm_x.shape, BF16),
            pltpu.VMEM(dy.shape, BF16),
            pltpu.VMEM(log_decay.shape[::-1], F32),
            pltpu.VMEM((4, 128, 128), BF16),
            pltpu.VMEM((2, 4, 128, 512), BF16),
            pltpu.VMEM((2, 4, 128, 512), BF16),
            pltpu.VMEM((2, 4, 128, 256), BF16),
            pltpu.VMEM((3, 8, 128), F32),
            pltpu.VMEM((2, 15, 8, 128), F32),
            pltpu.VMEM((2, 2, 2, 8, 128), F32),
            pltpu.VMEM((2, 2, 2, 8, 128), F32),
            pltpu.VMEM((7, 8, 128), F32),
            pltpu.VMEM((2, 128, 128), F32),
            pltpu.VMEM((2, 2, 2, 2, 128, 256), BF16),
            pltpu.VMEM((2, 2, 4, 256, 128), BF16),
            pltpu.VMEM((2, 2, 4, 256, 128), BF16),
            pltpu.VMEM((2, 2, 128, 128), BF16),
            pltpu.VMEM((2, 2, 128, 128), BF16),
            pltpu.VMEM((4, 2, 128, 256), BF16),
            pltpu.VMEM((4, 2, 128, 256), BF16),
            pltpu.VMEM((2, 128, 256), BF16),
            pltpu.SemaphoreType.DMA((N_SLOTS,)),
            pltpu.SemaphoreType.DMA((N_SLOTS,)),
            pltpu.SemaphoreType.DMA,
            pltpu.SemaphoreType.DMA((9,)),
        ],
        compiler_params=pltpu.CompilerParams(
            collective_id=0, has_side_effects=True, vmem_limit_bytes=63 * 1024 * 1024
        ),
        name="projection_backward",
    )(hidden, gain, proj_weight, b_c, ssm_x, dy, log_decay.T)
    return pl.pallas_call(
        hand_over,
        out_shape=tuple(jax.ShapeDtypeStruct(grad.shape, grad.dtype) for grad in grads),
        in_specs=[hbm] * 2,
        out_specs=(hbm, hbm),
        scratch_shapes=[
            pltpu.VMEM(hidden.shape, BF16),
            pltpu.VMEM(proj_weight.shape, BF16),
            pltpu.SemaphoreType.DMA((4,)),
        ],
        compiler_params=pltpu.CompilerParams(vmem_limit_bytes=63 * 1024 * 1024),
        name="hand_over",
    )(*grads)


def solution(mesh):
    return jax.shard_map(
        shards,
        mesh=mesh,
        in_specs=(
            P("dp", "tensor"),
            P("tensor"),
            P("dp", "tensor"),
            P("dp", "tensor"),
            P("dp", "tensor"),
            P("dp", "tensor"),
            P("dp", "tensor"),
        ),
        out_specs=(P("dp", "tensor"), P("dp", "tensor")),
        check_vma=False,
    )
```

time: 70.4 us -> 59.3 us (0.84)
  the two profiles are of different devices: /device:TPU:1 before, /device:TPU:9 now
where the time goes in v2:
time: 59.3 us; the launch traced here: 59.1 us
  Pallas kernels  58.5 us (99%)
  between operations  0.64 us (1%)
    pallas_call x1, Pallas kernels, shards(): pl.pallas_call(kernel, out_shape=(jax.ShapeDtypeStruct(hidden.shape, BF16...  56.8 us
    pallas_call x1, Pallas kernels, shards(): pl.pallas_call(hand_over, out_shape=tuple((jax.ShapeDtypeStruct(grad.shap...  1.66 us

profile of v2, /device:TPU:9, one launch (start us, length us, event | category | flops | bytes accessed | tf_op | source)
XLA Modules:
  0.0 59.1 jit_solution(7779724893008247076)
XLA Ops:
  0.6 56.8 %projection_backward.1 = (bf16[128,512]{1,0:T(8,128)(2,1)}, bf16[256,256]{1,0:T(8,128)(2,1)}) custom-call(bf16[128,512]{1,0:T(8,128)(2,1)} %hid_hbm.1, bf16[512]{0:T(512)(128)(2,1)} %gain_hbm.1, bf16[256,256]{1,0:T(8,128)(2,1)} %w_hbm.1, bf16[128,256]{1,0:T(8,128)(2,1)} %bc_hbm.1, bf16[128,1024]{1,0:T(8,128)(2,1)} %x_hbm.1, bf16[128,1024]{1,0:T(8,128)(2,1)} %dy_hbm.1, ...), custom_call_target="tpu_custom_call" | custom-call | tf_op jit(solution)/shard_map/projection_backward/pallas_call | solution.py:712
  57.4 1.7 %hand_over.1 = (bf16[128,512]{1,0:T(8,128)(2,1)}, bf16[256,256]{1,0:T(8,128)(2,1)}) custom-call(bf16[128,512]{1,0:T(8,128)(2,1)} %get-tuple-element.4.igrad_ref, bf16[256,256]{1,0:T(8,128)(2,1)} %get-tuple-element.5.wgrad_ref), custom_call_target="tpu_custom_call" | custom-call | tf_op jit(solution)/shard_map/hand_over/pallas_call | solution.py:758

commit v3 on v2

--- a/solution.py
+++ b/solution.py
@@ -94,6 +94,7 @@
     gsend,
     grecv,
     grelay,
+    prelay,
     ssem,
     rsem,
     lsem,
@@ -358,6 +359,57 @@
         d_y(dy).start()
     d_z(0).start()
     d_c(0, 0).start()
+    d_y(2).start()
+
+    def h_block(k, sy, sx):
+        lane = ((zb + k) % 2) * 256
+        return hall.at[sy, sx, :, pl.ds(pl.multiple_of(lane, 128), 256)]
+
+    def h_copy(k, n):
+        dx, fy = plane[n]
+        block = h_block(k, (yl + fy) % 2 if dx else yl, x)
+        dev = (za, zb, yh, (x + dx) % 4, yl if dx else 1 - yl, c)
+        return remote(block, block, S_HAG + 7 * k + n, dev)
+
+    def h_arrival(k, n):
+        sx, sy = plane_src(*plane[n])
+        block = h_block(k, sy, sx)
+        return remote(block, block, S_HAG + 7 * k + n, sibling)
+
+    def hid_on(k):
+        side = (zb + k) % 2
+        for u in range(2):
+
+            @pl.when(jnp.logical_not(hid_source_is_me(side, u)))
+            def _():
+                hid_arrival(side, u).wait_recv()
+
+        for n in (3, 0, 1):
+            h_copy(k, n).start()
+
+    def hid_across(k):
+        h_arrival(k, 3).wait_recv()
+        for n in (4, 5):
+            h_copy(k, n).start()
+
+    def hid_far(k, fy):
+        sx, sy = plane_src((1, 3)[k], fy)
+        block = h_block(k, sy, sx)
+        slot = S_HAG + 7 * k + 2 + 4 * fy
+        return remote(block, block, slot, (za, zb, yh, (x + (1, 3)[k]) % 4, yl, c))
+
+    def hid_relay(k, fy):
+        h_arrival(k, k + 4 * fy).wait_recv()
+        hid_far(k, fy).start()
+
+    hid_on(0)
+    hid_on(1)
+
+    def d_on(dy):
+        d_y_arrival(dy).wait_recv()
+        if dy != 2:
+            d_z(dy).start()
+        d_c(0, dy).start()
 
     square = sums[1]
     for n in range(7):
@@ -379,59 +431,20 @@
     for n in range(7):
         inv_copy(n).start()
 
-    def h_block(k, sy, sx):
-        lane = ((zb + k) % 2) * 256
-        return hall.at[sy, sx, :, pl.ds(pl.multiple_of(lane, 128), 256)]
-
-    def h_copy(k, n):
-        dx, fy = plane[n]
-        block = h_block(k, (yl + fy) % 2 if dx else yl, x)
-        dev = (za, zb, yh, (x + dx) % 4, yl if dx else 1 - yl, c)
-        return remote(block, block, S_HAG + 7 * k + n, dev)
-
-    def h_arrival(k, n):
-        sx, sy = plane_src(*plane[n])
-        block = h_block(k, sy, sx)
-        return remote(block, block, S_HAG + 7 * k + n, sibling)
-
-    def hid_on(k):
-        side = (zb + k) % 2
-        for u in range(2):
-
-            @pl.when(jnp.logical_not(hid_source_is_me(side, u)))
-            def _():
-                hid_arrival(side, u).wait_recv()
-
-        for n in (3, 0, 1, 2):
-            h_copy(k, n).start()
-
-    def hid_across(k):
-        h_arrival(k, 3).wait_recv()
-        for n in range(4, 7):
-            h_copy(k, n).start()
-
-    hid_on(0)
-    hid_on(1)
-    d_y(2).start()
-
-    def d_on(dy):
-        d_y_arrival(dy).wait_recv()
-        if dy != 2:
-            d_z(dy).start()
-        d_c(0, dy).start()
-
     d_on(1)
     d_on(3)
-    hid_across(0)
-    d_z_arrival(0).wait_recv()
-    d_z(2).start()
-    d_c(1, 0).start()
     for n in range(4):
         w_arrival(n).wait_recv()
     for j in range(2):
         w_on(j).start()
+    d_z_arrival(0).wait_recv()
+    d_z(2).start()
+    d_c(1, 0).start()
+    hid_across(0)
+    hid_relay(0, 0)
+    hid_relay(1, 0)
+    d_on(2)
     hid_across(1)
-    d_on(2)
 
     for dy in (0, 1, 3, 2):
         d_c_arrival(0, dy).wait_recv()
@@ -439,8 +452,9 @@
     def p_copy(k, n):
         dx, fy = plane[n]
         side = (zb + k) % 2
+        relayed = k == 0 and (dx, fy) in ((1, 0), (3, 1))
         return remote(
-            psend.at[side, (yl + fy) % 2, (x + dx) % 4],
+            prelay.at[fy] if relayed else psend.at[side, (yl + fy) % 2, (x + dx) % 4],
             precv.at[side, yl, x],
             S_P + 7 * k + n,
             plane_dev(dx, fy),
@@ -458,12 +472,29 @@
             out = out + nt_dot(dall[1, py, side].reshape(256, 256), wall[1, tx])
             psend[side, py, tx] = out.astype(BF16)
 
+    def p_far(fy):
+        block = psend.at[zb, (yl + fy) % 2, (x + 2) % 4]
+        dev = (za, zb, yh, (x + (1, 3)[fy]) % 4, yl, c)
+        return remote(block, prelay.at[fy], S_P + 2 + 4 * fy, dev)
+
+    def p_relay(fy):
+        p_far(fy).wait_recv()
+        to = (yl + fy) % 2, (x + (1, 3)[fy]) % 4
+        own = psend[(zb,) + to].astype(F32)
+        prelay[fy] = (own + prelay[fy].astype(F32)).astype(BF16)
+        p_copy(0, 5 * fy).start()
+
     def p_start(k, dza):
         for n, (dx, fy) in enumerate(plane):
+            if (dx, fy) in ((1, 0), (3, 1)):
+                continue
 
             @pl.when((x + dx) % 4 == (za + dza) % 4)
             def _():
-                p_copy(k, n).start()
+                if dx == 2:
+                    p_far(fy).start()
+                else:
+                    p_copy(k, n).start()
 
     w_arrival(4).wait_recv()
     terms(0, 0)
@@ -472,10 +503,12 @@
     p_start(0, 1)
     terms(0, 3)
     p_start(0, 3)
+    hid_relay(0, 1)
     for j in range(2):
         w_on_arrival(j).wait_recv()
     terms(0, 2)
     p_start(0, 2)
+    hid_relay(1, 1)
     for dy in (1, 3, 2):
         d_z_arrival(dy).wait_recv()
         d_c(1, dy).start()
@@ -518,11 +551,15 @@
         row = other_inv if fy else own_inv
         hscaled[sy, sx] = (hall[sy, sx].astype(F32) * row).astype(BF16)
 
+    p_relay(0)
+    p_relay(1)
+
     scale(0, 0)
     scale(0, 1)
-    for n in (0, 1, 2, 4, 5, 6):
-        h_arrival(0, n).wait_recv()
-        h_arrival(1, n).wait_recv()
+    for n in (0, 1, 4, 5, 2, 6):
+        for k in range(2):
+            if n % 4 != k:
+                h_arrival(k, n).wait_recv()
         scale(*plane[n])
     eye = (rows == cols).astype(F32)
     for py in range(2):
@@ -548,16 +585,21 @@
     for n in range(7):
         p_copy(1, n).start()
 
+    def g_terms(first, count, j):
+        rows = [hscaled[sy, pl.ds(first, count)].reshape(count * 128, 512) for sy in range(2)]
+        out = nn_dot(rows[0], dall[j, 0].reshape(512, 256))
+        out = out + nn_dot(rows[1], dall[j, 1].reshape(512, 256))
+        gsend[pl.ds(first, count), j] = out.astype(BF16).reshape(count, 128, 256)
+
     for j in range(2):
-        out = nn_dot(hscaled[0].reshape(512, 512), dall[j, 0].reshape(512, 256))
-        out = out + nn_dot(hscaled[1].reshape(512, 512), dall[j, 1].reshape(512, 256))
-        out = out.astype(BF16)
-        for k in range(4):
-            gsend[k, j] = out[k * 128 : (k + 1) * 128, :]
+        g_terms((za + 2) % 4, 1, j)
+        g_relay(j).start()
     for j in range(2):
-        g_relay(j).start()
-    g_copy(0, 1).start()
-    g_copy(1, 0).start()
+        g_terms((za + (3, 1)[j]) % 4, 1, j)
+        g_copy(1 - j, j).start()
+    for j in range(2):
+        g_terms((za + (1, 3)[j]) % 4, 1, j)
+        g_terms(za, 1, j)
     g_sibling().start()
 
     def q_copy(k, u):
@@ -572,10 +614,11 @@
 
     def owners(k):
         side = (zb + k) % 2
-        for n in range(7):
+        arrivals = (1, 4, 3, 0, 5) if k == 0 else range(7)
+        for n in arrivals:
             p_arrival(k, n).wait_recv()
         acc = psend[side, yl, x].astype(F32)
-        for n in range(7):
+        for n in arrivals:
             sx, sy = plane_src(*plane[n])
             acc = acc + precv[side, sy, sx].astype(F32)
         rsum[side] = acc.astype(BF16).reshape(2, 128, 128)
@@ -591,21 +634,21 @@
                 own.start()
                 own.wait()
 
-    owners(0)
+    for n in range(7):
+        dot_copy(n).wait_recv()
+    value = dots[seq(zb, yh)]
+    for n in range(7):
+        value = value + dots_in[n]
+    sums[2] = value
+    for n in range(15):
+        mean_copy(n).start()
     for j in range(2):
         g_relay(j).wait_recv()
         to = (za + (1, 3)[j]) % 4
         gsend[to, j] = (gsend[to, j].astype(F32) + grelay[j].astype(F32)).astype(BF16)
         g_copy(j, j).start()
 
-    for n in range(7):
-        dot_copy(n).wait_recv()
-    value = dots[seq(zb, yh)]
-    for n in range(7):
-        value = value + dots_in[n]
-    sums[2] = value
-    for n in range(15):
-        mean_copy(n).start()
+    owners(0)
     owners(1)
 
     g_sibling().wait_recv()
@@ -673,9 +716,15 @@
         for d in range(2):
             g_copy(d, j).wait_send()
     for n in range(7):
-        h_copy(0, n).wait_send()
-        h_copy(1, n).wait_send()
-        p_copy(0, n).wait_send()
+        for k in range(2):
+            if n % 4 != 2:
+                h_copy(k, n).wait_send()
+            else:
+                hid_far(k, n // 4).wait_send()
+        if n % 4 != 2:
+            p_copy(0, n).wait_send()
+        else:
+            p_far(n // 4).wait_send()
         p_copy(1, n).wait_send()
         inv_copy(n).wait_send()
         dot_copy(n).wait_send()
@@ -745,6 +794,7 @@
             pltpu.VMEM((4, 2, 128, 256), BF16),
             pltpu.VMEM((4, 2, 128, 256), BF16),
             pltpu.VMEM((2, 128, 256), BF16),
+            pltpu.VMEM((2, 256, 128), BF16),
             pltpu.SemaphoreType.DMA((N_SLOTS,)),
             pltpu.SemaphoreType.DMA((N_SLOTS,)),
             pltpu.SemaphoreType.DMA,

time: 59.3 us -> 57.6 us (0.971)
  the two profiles are of different devices: /device:TPU:9 before, /device:TPU:1 now
where the time goes in v3:
time: 57.6 us; the launch traced here: 57.2 us
  Pallas kernels  56.5 us (98%)
  between operations  0.64 us (1%)
    pallas_call x1, Pallas kernels, shards(): pl.pallas_call(kernel, out_shape=(jax.ShapeDtypeStruct(hidden.shape, BF16...  54.9 us
    pallas_call x1, Pallas kernels, shards(): pl.pallas_call(hand_over, out_shape=tuple((jax.ShapeDtypeStruct(grad.shap...  1.66 us

profile of v3, /device:TPU:1, one launch (start us, length us, event | category | flops | bytes accessed | tf_op | source)
XLA Modules:
  0.0 57.2 jit_solution(12021705980343649990)
XLA Ops:
  0.6 54.9 %projection_backward.1 = (bf16[128,512]{1,0:T(8,128)(2,1)}, bf16[256,256]{1,0:T(8,128)(2,1)}) custom-call(bf16[128,512]{1,0:T(8,128)(2,1)} %hid_hbm.1, bf16[512]{0:T(512)(128)(2,1)} %gain_hbm.1, bf16[256,256]{1,0:T(8,128)(2,1)} %w_hbm.1, bf16[128,256]{1,0:T(8,128)(2,1)} %bc_hbm.1, bf16[128,1024]{1,0:T(8,128)(2,1)} %x_hbm.1, bf16[128,1024]{1,0:T(8,128)(2,1)} %dy_hbm.1, ...), custom_call_target="tpu_custom_call" | custom-call | tf_op jit(solution)/shard_map/projection_backward/pallas_call | solution.py:761
  55.5 1.7 %hand_over.1 = (bf16[128,512]{1,0:T(8,128)(2,1)}, bf16[256,256]{1,0:T(8,128)(2,1)}) custom-call(bf16[128,512]{1,0:T(8,128)(2,1)} %get-tuple-element.4.igrad_ref, bf16[256,256]{1,0:T(8,128)(2,1)} %get-tuple-element.5.wgrad_ref), custom_call_target="tpu_custom_call" | custom-call | tf_op jit(solution)/shard_map/hand_over/pallas_call | solution.py:808

commit v4 on v3

--- a/solution.py
+++ b/solution.py
@@ -51,7 +51,9 @@
 S_DC = SLOTS.take(8)
 S_P = SLOTS.take(14)
 S_Q = SLOTS.take(4)
-S_G = SLOTS.take(7)
+S_G = SLOTS.take(3)
+S_GIN = SLOTS.take(4)
+S_GON = SLOTS.take(4)
 S_DOT = SLOTS.take(8)
 S_MEAN = SLOTS.take(15)
 N_SLOTS = SLOTS.count
@@ -230,7 +232,7 @@
         ht[k] = scaled[:, k * 128 : (k + 1) * 128].T.astype(BF16)
 
     def row_of(column):
-        return jnp.broadcast_to(column, (128, 128)).T[0:8, :]
+        return jnp.broadcast_to(column, (128, 128)).T[0:1, :]
 
     def column_of(row):
         return jnp.broadcast_to(row[0:1, :], (128, 128)).T
@@ -332,6 +334,16 @@
         block = dall.at[(c,) + seq(zb, yh)]
         return remote(block, block, S_DY + dy, column_dev(0, dy))
 
+    def d_far(dy):
+        half = slice(0, 64) if dy == 1 else slice(64, 128)
+        block = dall.at[(c,) + seq(zb, (yh + 4 - dy) % 4) + (half,)]
+        return remote(block, block, S_DY + dy - 1, column_dev(0, dy))
+
+    def d_far_arrival(dy):
+        half = slice(0, 64) if dy == 1 else slice(64, 128)
+        block = dall.at[(c,) + seq(zb, (yh + 2) % 4) + (half,)]
+        return remote(block, block, S_DY + dy - 1, sibling)
+
     def d_y_arrival(dy):
         block = dall.at[(c,) + seq(zb, (yh + 4 - dy) % 4)]
         return remote(block, block, S_DY + dy, sibling)
@@ -359,7 +371,6 @@
         d_y(dy).start()
     d_z(0).start()
     d_c(0, 0).start()
-    d_y(2).start()
 
     def h_block(k, sy, sx):
         lane = ((zb + k) % 2) * 256
@@ -406,8 +417,12 @@
     hid_on(1)
 
     def d_on(dy):
-        d_y_arrival(dy).wait_recv()
-        if dy != 2:
+        if dy == 2:
+            d_far_arrival(1).wait_recv()
+            d_far_arrival(3).wait_recv()
+        else:
+            d_y_arrival(dy).wait_recv()
+            d_far(dy).start()
             d_z(dy).start()
         d_c(0, dy).start()
 
@@ -517,24 +532,46 @@
     for dza in range(4):
         terms(1, dza)
 
-    def g_copy(d, j):
-        dza = (1, 3)[d]
-        dev = ((za + dza) % 4, zb, yh, x, yl, j)
+    def g_dev(dza, j):
+        return ((za + dza) % 4, zb, yh, x, yl, j)
+
+    def g_copy(j):
+        dza = (3, 1)[j]
         return remote(
-            gsend.at[(za + dza) % 4, j], grecv.at[za, c], S_G + 2 * d + j, dev, S_G + 2 * d + c
-        )
-
-    def g_arrival(d, h):
-        block = grecv.at[(za + (3, 1)[d]) % 4, h]
-        return remote(block, block, S_G + 2 * d + h, sibling)
+            gsend.at[(za + dza) % 4, j], grecv.at[za, c], S_G + j, g_dev(dza, j), S_G + c
+        )
+
+    def g_arrival(h):
+        block = grecv.at[jnp.where(c == 0, (za + 1) % 4, (za + 3) % 4), h]
+        return remote(block, block, S_G + h, sibling)
 
     def g_sibling():
-        return remote(gsend.at[za, 1 - c], grecv.at[za, c], S_G + 4, sibling)
-
-    def g_relay(j):
+        return remote(gsend.at[za, 1 - c], grecv.at[za, c], S_G + 2, sibling)
+
+    def g_relay(j, part):
+        half = slice(part * 64, part * 64 + 64)
         return remote(
-            gsend.at[(za + 2) % 4, j], grelay.at[j], S_G + 5 + j, far((1, 3)[j], 0)
-        )
+            gsend.at[(za + 2) % 4, j, half],
+            grelay.at[j, half],
+            S_GIN + 2 * j + part,
+            g_dev((1, 3)[j], c),
+        )
+
+    def g_on(j, part):
+        dza = (1, 3)[j]
+        half = slice(part * 64, part * 64 + 64)
+        return remote(
+            gsend.at[(za + dza) % 4, j, half],
+            grecv.at[za, c, half],
+            S_GON + 2 * j + part,
+            g_dev(dza, j),
+            S_GON + 2 * c + part,
+        )
+
+    def g_on_arrival(h, part):
+        half = slice(part * 64, part * 64 + 64)
+        block = grecv.at[jnp.where(c == 0, (za + 3) % 4, (za + 1) % 4), h, half]
+        return remote(block, block, S_GON + 2 * h + part, sibling)
 
     for n in range(7):
         inv_arrival(n).wait_recv()
@@ -573,7 +610,7 @@
                         psend[side, py, f, part, :], hall[py, f, :, lane : lane + 128]
                     )
                 row = jnp.sum(prod * eye, axis=0, keepdims=True)
-                dots[py, side, u] = jnp.broadcast_to(row, (8, 128))
+                dots[py, side, u] = row
 
     def dot_copy(n):
         k, dy = column[n]
@@ -593,10 +630,12 @@
 
     for j in range(2):
         g_terms((za + 2) % 4, 1, j)
-        g_relay(j).start()
+        g_relay(j, 0).start()
+    for j in range(2):
+        g_relay(j, 1).start()
     for j in range(2):
         g_terms((za + (3, 1)[j]) % 4, 1, j)
-        g_copy(1 - j, j).start()
+        g_copy(j).start()
     for j in range(2):
         g_terms((za + (1, 3)[j]) % 4, 1, j)
         g_terms(za, 1, j)
@@ -634,6 +673,16 @@
                 own.start()
                 own.wait()
 
+    def g_relays(part):
+        half = slice(part * 64, part * 64 + 64)
+        for j in range(2):
+            g_relay(j, part).wait_recv()
+            to = (za + (1, 3)[j]) % 4
+            own = gsend[to, j, half].astype(F32)
+            gsend[to, j, half] = (own + grelay[j, half].astype(F32)).astype(BF16)
+            g_on(j, part).start()
+
+    g_relays(0)
     for n in range(7):
         dot_copy(n).wait_recv()
     value = dots[seq(zb, yh)]
@@ -642,19 +691,16 @@
     sums[2] = value
     for n in range(15):
         mean_copy(n).start()
-    for j in range(2):
-        g_relay(j).wait_recv()
-        to = (za + (1, 3)[j]) % 4
-        gsend[to, j] = (gsend[to, j].astype(F32) + grelay[j].astype(F32)).astype(BF16)
-        g_copy(j, j).start()
+    g_relays(1)
 
     owners(0)
     owners(1)
 
     g_sibling().wait_recv()
     for h in range(2):
-        for d in range(2):
-            g_arrival(d, h).wait_recv()
+        g_arrival(h).wait_recv()
+        for part in range(2):
+            g_on_arrival(h, part).wait_recv()
     grecv[za, c] = gsend[za, c]
     for h in range(2):
         acc = grecv[za, h].astype(F32)
@@ -712,9 +758,10 @@
     g_sibling().wait_send()
     for j in range(2):
         w_on(j).wait_send()
-        g_relay(j).wait_send()
-        for d in range(2):
-            g_copy(d, j).wait_send()
+        g_copy(j).wait_send()
+        for part in range(2):
+            g_relay(j, part).wait_send()
+            g_on(j, part).wait_send()
     for n in range(7):
         for k in range(2):
             if n % 4 != 2:
@@ -729,8 +776,9 @@
         inv_copy(n).wait_send()
         dot_copy(n).wait_send()
     for dy in range(4):
-        if dy:
+        if dy % 2:
             d_y(dy).wait_send()
+            d_far(dy).wait_send()
         d_z(dy).wait_send()
         d_c(0, dy).wait_send()
         d_c(1, dy).wait_send()
@@ -780,11 +828,11 @@
             pltpu.VMEM((2, 4, 128, 512), BF16),
             pltpu.VMEM((2, 4, 128, 512), BF16),
             pltpu.VMEM((2, 4, 128, 256), BF16),
-            pltpu.VMEM((3, 8, 128), F32),
-            pltpu.VMEM((2, 15, 8, 128), F32),
-            pltpu.VMEM((2, 2, 2, 8, 128), F32),
-            pltpu.VMEM((2, 2, 2, 8, 128), F32),
-            pltpu.VMEM((7, 8, 128), F32),
+            pltpu.VMEM((3, 1, 128), F32),
+            pltpu.VMEM((2, 15, 1, 128), F32),
+            pltpu.VMEM((2, 2, 2, 1, 128), F32),
+            pltpu.VMEM((2, 2, 2, 1, 128), F32),
+            pltpu.VMEM((7, 1, 128), F32),
             pltpu.VMEM((2, 128, 128), F32),
             pltpu.VMEM((2, 2, 2, 2, 128, 256), BF16),
             pltpu.VMEM((2, 2, 4, 256, 128), BF16),

time: 57.6 us -> 56.6 us (0.983)
  the two profiles are of different devices: /device:TPU:1 before, /device:TPU:8 now
where the time goes in v4:
time: 56.6 us; the launch traced here: 56.4 us
  Pallas kernels  55.8 us (99%)
  between operations  0.64 us (1%)
    pallas_call x1, Pallas kernels, shards(): pl.pallas_call(kernel, out_shape=(jax.ShapeDtypeStruct(hidden.shape, BF16...  54.1 us
    pallas_call x1, Pallas kernels, shards(): pl.pallas_call(hand_over, out_shape=tuple((jax.ShapeDtypeStruct(grad.shap...  1.66 us

profile of v4, /device:TPU:8, one launch (start us, length us, event | category | flops | bytes accessed | tf_op | source)
XLA Modules:
  0.0 56.4 jit_solution(11133214986971801751)
XLA Ops:
  0.6 54.1 %projection_backward.1 = (bf16[128,512]{1,0:T(8,128)(2,1)}, bf16[256,256]{1,0:T(8,128)(2,1)}) custom-call(bf16[128,512]{1,0:T(8,128)(2,1)} %hid_hbm.1, bf16[512]{0:T(512)(128)(2,1)} %gain_hbm.1, bf16[256,256]{1,0:T(8,128)(2,1)} %w_hbm.1, bf16[128,256]{1,0:T(8,128)(2,1)} %bc_hbm.1, bf16[128,1024]{1,0:T(8,128)(2,1)} %x_hbm.1, bf16[128,1024]{1,0:T(8,128)(2,1)} %dy_hbm.1, ...), custom_call_target="tpu_custom_call" | custom-call | tf_op jit(solution)/shard_map/projection_backward/pallas_call | solution.py:809
  54.8 1.7 %hand_over.1 = (bf16[128,512]{1,0:T(8,128)(2,1)}, bf16[256,256]{1,0:T(8,128)(2,1)}) custom-call(bf16[128,512]{1,0:T(8,128)(2,1)} %get-tuple-element.4.igrad_ref, bf16[256,256]{1,0:T(8,128)(2,1)} %get-tuple-element.5.wgrad_ref), custom_call_target="tpu_custom_call" | custom-call | tf_op jit(solution)/shard_map/hand_over/pallas_call | solution.py:856

commit v5 on v4

--- a/solution.py
+++ b/solution.py
@@ -106,12 +106,12 @@
         pltpu.make_async_copy(src, dst, isem.at[n])
         for n, (src, dst) in enumerate(
             (
+                (hid_hbm, hid_ref),
+                (gain_hbm, gain_ref),
+                (w_hbm, w_ref),
                 (ld_hbm, ld_ref),
                 (x_hbm, x_ref),
                 (dy_hbm, dy_ref),
-                (hid_hbm, hid_ref),
-                (gain_hbm, gain_ref),
-                (w_hbm, w_ref),
                 (bc_hbm, bc_ref),
             )
         )
@@ -201,6 +201,98 @@
     own_hop = jnp.where((yl == zb) & (yl == yh % 2) & (c == yh // 2), 1, 0)
 
     for load in loads[:3]:
+        load.wait()
+    hid = hid_ref[...].astype(F32)
+    gain = gain_ref[...].astype(F32).reshape(1, -1)
+    scaled = hid * gain
+    for k in range(4):
+        ht[k] = scaled[:, k * 128 : (k + 1) * 128].T.astype(BF16)
+
+    def row_of(column):
+        return jnp.broadcast_to(column, (128, 128)).T[0:1, :]
+
+    def column_of(row):
+        return jnp.broadcast_to(row[0:1, :], (128, 128)).T
+
+    sums[0] = row_of(jnp.sum(hid * hid, axis=1, keepdims=True))
+    wall[c, za] = w_ref[pl.ds(pl.multiple_of(c * 128, 128), 128), :]
+
+    pl.semaphore_wait(barrier, met + 8 - 2 * own_hop)
+
+    sq_sibling = remote(sums.at[0], sums_in.at[0, 0], S_SQ, sibling)
+    sq_sibling.start()
+
+    def sq_copy(n):
+        return remote(sums.at[1], sums_in.at[0, 1 + n], S_SQ + 1 + n, plane_dev(*plane[n]))
+
+    def mean_copy(n):
+        return remote(sums.at[2], sums_in.at[1, n], S_MEAN + n, tensor_dev(*tensor[n]))
+
+    def hid_copy(i, h):
+        lane = (2 * zb + yh // 2) * 128
+        return remote(
+            ht.at[2 * i + h],
+            hall.at[yh % 2, x, :, pl.ds(pl.multiple_of(lane, 128), 128)],
+            S_HID + 2 * i + h,
+            hid_target(i, h),
+            S_HID + 2 * zb + yh // 2,
+        )
+
+    def hid_arrival(side, u):
+        lane = (2 * side + u) * 128
+        return remote(
+            ht.at[0],
+            hall.at[yl, x, :, pl.ds(pl.multiple_of(lane, 128), 128)],
+            S_HID + 2 * side + u,
+            sibling,
+        )
+
+    for i in range(2):
+        for h in range(2):
+
+            @pl.when(jnp.logical_not(hid_target_is_me(i, h)))
+            def _():
+                hid_copy(i, h).start()
+
+            @pl.when(hid_target_is_me(i, h))
+            def _():
+                lane = (2 * zb + yh // 2) * 128
+                own = pltpu.make_async_copy(
+                    ht.at[2 * i + h],
+                    hall.at[yl, x, :, pl.ds(pl.multiple_of(lane, 128), 128)],
+                    lsem,
+                )
+                own.start()
+                own.wait()
+
+    def w_copy(n):
+        dza, fc = depth[n]
+        core = (c + fc) % 2
+        return remote(
+            w_ref.at[pl.ds(pl.multiple_of(core * 128, 128), 128), :],
+            wall.at[c, za],
+            S_W + n,
+            far(dza, fc),
+        )
+
+    def w_arrival(n):
+        dza, fc = depth[n]
+        return remote(
+            w_ref.at[0:128, :], wall.at[(c + fc) % 2, (za + 4 - dza) % 4], S_W + n, sibling
+        )
+
+    for n in range(5):
+        w_copy(n).start()
+
+    def w_on(j):
+        block = wall.at[j, (za + (1, 3)[j] + 2) % 4]
+        return remote(block, block, S_W + 5 + j, far((1, 3)[j], 0))
+
+    def w_on_arrival(j):
+        block = wall.at[j, (za + 2) % 4]
+        return remote(block, block, S_W + 5 + j, sibling)
+
+    for load in loads[3:]:
         load.wait()
     rows = lax.broadcasted_iota(jnp.int32, (128, 128), 0)
     cols = lax.broadcasted_iota(jnp.int32, (128, 128), 1)
@@ -223,100 +315,8 @@
             total = total + inner[:, k * 128 : (k + 1) * 128] * decay
     gram[0] = total
 
-    for load in loads[3:]:
-        load.wait()
-    hid = hid_ref[...].astype(F32)
-    gain = gain_ref[...].astype(F32).reshape(1, -1)
-    scaled = hid * gain
-    for k in range(4):
-        ht[k] = scaled[:, k * 128 : (k + 1) * 128].T.astype(BF16)
-
-    def row_of(column):
-        return jnp.broadcast_to(column, (128, 128)).T[0:1, :]
-
-    def column_of(row):
-        return jnp.broadcast_to(row[0:1, :], (128, 128)).T
-
-    sums[0] = row_of(jnp.sum(hid * hid, axis=1, keepdims=True))
-    wall[c, za] = w_ref[pl.ds(pl.multiple_of(c * 128, 128), 128), :]
-
-    pl.semaphore_wait(barrier, met + 8 - 2 * own_hop)
-
     gram_copy = remote(gram.at[0], gram.at[1], S_GRAM, sibling)
     gram_copy.start()
-
-    sq_sibling = remote(sums.at[0], sums_in.at[0, 0], S_SQ, sibling)
-    sq_sibling.start()
-
-    def sq_copy(n):
-        return remote(sums.at[1], sums_in.at[0, 1 + n], S_SQ + 1 + n, plane_dev(*plane[n]))
-
-    def mean_copy(n):
-        return remote(sums.at[2], sums_in.at[1, n], S_MEAN + n, tensor_dev(*tensor[n]))
-
-    def hid_copy(i, h):
-        lane = (2 * zb + yh // 2) * 128
-        return remote(
-            ht.at[2 * i + h],
-            hall.at[yh % 2, x, :, pl.ds(pl.multiple_of(lane, 128), 128)],
-            S_HID + 2 * i + h,
-            hid_target(i, h),
-            S_HID + 2 * zb + yh // 2,
-        )
-
-    def hid_arrival(side, u):
-        lane = (2 * side + u) * 128
-        return remote(
-            ht.at[0],
-            hall.at[yl, x, :, pl.ds(pl.multiple_of(lane, 128), 128)],
-            S_HID + 2 * side + u,
-            sibling,
-        )
-
-    for i in range(2):
-        for h in range(2):
-
-            @pl.when(jnp.logical_not(hid_target_is_me(i, h)))
-            def _():
-                hid_copy(i, h).start()
-
-            @pl.when(hid_target_is_me(i, h))
-            def _():
-                lane = (2 * zb + yh // 2) * 128
-                own = pltpu.make_async_copy(
-                    ht.at[2 * i + h],
-                    hall.at[yl, x, :, pl.ds(pl.multiple_of(lane, 128), 128)],
-                    lsem,
-                )
-                own.start()
-                own.wait()
-
-    def w_copy(n):
-        dza, fc = depth[n]
-        core = (c + fc) % 2
-        return remote(
-            w_ref.at[pl.ds(pl.multiple_of(core * 128, 128), 128), :],
-            wall.at[c, za],
-            S_W + n,
-            far(dza, fc),
-        )
-
-    def w_arrival(n):
-        dza, fc = depth[n]
-        return remote(
-            w_ref.at[0:128, :], wall.at[(c + fc) % 2, (za + 4 - dza) % 4], S_W + n, sibling
-        )
-
-    for n in range(5):
-        w_copy(n).start()
-
-    def w_on(j):
-        block = wall.at[j, (za + (1, 3)[j] + 2) % 4]
-        return remote(block, block, S_W + 5 + j, far((1, 3)[j], 0))
-
-    def w_on_arrival(j):
-        block = wall.at[j, (za + 2) % 4]
-        return remote(block, block, S_W + 5 + j, sibling)
 
     sq_sibling.wait_recv()
     sums[1] = sums[0] + sums_in[0, 0]
@@ -458,9 +458,9 @@
     hid_across(0)
     hid_relay(0, 0)
     hid_relay(1, 0)
+    hid_across(1)
+
     d_on(2)
-    hid_across(1)
-
     for dy in (0, 1, 3, 2):
         d_c_arrival(0, dy).wait_recv()
 
@@ -512,18 +512,16 @@
                     p_copy(k, n).start()
 
     w_arrival(4).wait_recv()
-    terms(0, 0)
-    p_start(0, 0)
-    terms(0, 1)
-    p_start(0, 1)
-    terms(0, 3)
-    p_start(0, 3)
+    for dza in (0, 1, 3):
+        terms(0, dza)
     hid_relay(0, 1)
+    hid_relay(1, 1)
+    for dza in (0, 1, 3):
+        p_start(0, dza)
     for j in range(2):
         w_on_arrival(j).wait_recv()
     terms(0, 2)
     p_start(0, 2)
-    hid_relay(1, 1)
     for dy in (1, 3, 2):
         d_z_arrival(dy).wait_recv()
         d_c(1, dy).start()
@@ -587,9 +585,6 @@
         sx, sy = plane_src(dx, fy)
         row = other_inv if fy else own_inv
         hscaled[sy, sx] = (hall[sy, sx].astype(F32) * row).astype(BF16)
-
-    p_relay(0)
-    p_relay(1)
 
     scale(0, 0)
     scale(0, 1)
@@ -619,6 +614,8 @@
 
     for n in range(7):
         dot_copy(n).start()
+    p_relay(0)
+    p_relay(1)
     for n in range(7):
         p_copy(1, n).start()
 

time: 56.6 us -> 56.5 us (level)
  the two profiles are of different devices: /device:TPU:8 before, /device:TPU:1 now
where the time goes in v5:
time: 56.5 us; the launch traced here: 55.9 us
  Pallas kernels  55.2 us (98%)
  between operations  0.64 us (1%)
    pallas_call x1, Pallas kernels, shards(): pl.pallas_call(kernel, out_shape=(jax.ShapeDtypeStruct(hidden.shape, BF16...  53.6 us
    pallas_call x1, Pallas kernels, shards(): pl.pallas_call(hand_over, out_shape=tuple((jax.ShapeDtypeStruct(grad.shap...  1.66 us

profile of v5, /device:TPU:1, one launch (start us, length us, event | category | flops | bytes accessed | tf_op | source)
XLA Modules:
  0.0 55.9 jit_solution(6801606083425356837)
XLA Ops:
  0.6 53.6 %projection_backward.1 = (bf16[128,512]{1,0:T(8,128)(2,1)}, bf16[256,256]{1,0:T(8,128)(2,1)}) custom-call(bf16[128,512]{1,0:T(8,128)(2,1)} %hid_hbm.1, bf16[512]{0:T(512)(128)(2,1)} %gain_hbm.1, bf16[256,256]{1,0:T(8,128)(2,1)} %w_hbm.1, bf16[128,256]{1,0:T(8,128)(2,1)} %bc_hbm.1, bf16[128,1024]{1,0:T(8,128)(2,1)} %x_hbm.1, bf16[128,1024]{1,0:T(8,128)(2,1)} %dy_hbm.1, ...), custom_call_target="tpu_custom_call" | custom-call | tf_op jit(solution)/shard_map/projection_backward/pallas_call | solution.py:806
  54.2 1.7 %hand_over.1 = (bf16[128,512]{1,0:T(8,128)(2,1)}, bf16[256,256]{1,0:T(8,128)(2,1)}) custom-call(bf16[128,512]{1,0:T(8,128)(2,1)} %get-tuple-element.4.igrad_ref, bf16[256,256]{1,0:T(8,128)(2,1)} %get-tuple-element.5.wgrad_ref), custom_call_target="tpu_custom_call" | custom-call | tf_op jit(solution)/shard_map/hand_over/pallas_call | solution.py:853

commit v6 on v5

--- a/solution.py
+++ b/solution.py
@@ -55,7 +55,7 @@
 S_GIN = SLOTS.take(4)
 S_GON = SLOTS.take(4)
 S_DOT = SLOTS.take(8)
-S_MEAN = SLOTS.take(15)
+S_MEAN = SLOTS.take(8)
 N_SLOTS = SLOTS.count
 
 
@@ -140,7 +140,6 @@
     plane = [(1, 0), (3, 0), (2, 0), (0, 1), (1, 1), (3, 1), (2, 1)]
     column = [(0, 1), (0, 3), (0, 2), (1, 0), (1, 1), (1, 3), (1, 2)]
     depth = [(dza, fc) for dza in (1, 3) for fc in range(2)] + [(0, 1)]
-    tensor = [(0, 0, 1)] + [(dx, fy, fc) for fc in range(2) for dx, fy in plane]
 
     def plane_dev(dx, fy):
         return (za, zb, yh, (x + dx) % 4, (yl + fy) % 2, c)
@@ -148,9 +147,6 @@
     def plane_src(dx, fy):
         return (x + 4 - dx) % 4, (yl + fy) % 2
 
-    def tensor_dev(dx, fy, fc):
-        return (za, zb, yh, (x + dx) % 4, (yl + fy) % 2, (c + fc) % 2)
-
     def column_dev(k, dy):
         return (za, (zb + k) % 2, (yh + dy) % 4, x, yl, c)
 
@@ -177,13 +173,14 @@
     def greet(dev):
         pl.semaphore_signal(barrier, inc=1, device_id=device(*dev), device_id_type=MESH)
 
-    for dx, fy, fc in tensor:
-        greet(tensor_dev(dx, fy, fc))
+    greet(sibling)
+    for dx, fy in plane:
+        greet(plane_dev(dx, fy))
     for k, dy in column:
         greet(column_dev(k, dy))
     for dza, fc in depth[:-1]:
         greet(far(dza, fc))
-    met = 15 + 7 + 4
+    met = 8 + 7 + 4
     for i in range(2):
         for h in range(2):
 
@@ -225,8 +222,10 @@
     def sq_copy(n):
         return remote(sums.at[1], sums_in.at[0, 1 + n], S_SQ + 1 + n, plane_dev(*plane[n]))
 
+    mean_sibling = remote(sums.at[2], sums_in.at[1, 0], S_MEAN, sibling)
+
     def mean_copy(n):
-        return remote(sums.at[2], sums_in.at[1, n], S_MEAN + n, tensor_dev(*tensor[n]))
+        return remote(sums.at[3], sums_in.at[1, 1 + n], S_MEAN + 1 + n, plane_dev(*plane[n]))
 
     def hid_copy(i, h):
         lane = (2 * zb + yh // 2) * 128
@@ -614,11 +613,6 @@
 
     for n in range(7):
         dot_copy(n).start()
-    p_relay(0)
-    p_relay(1)
-    for n in range(7):
-        p_copy(1, n).start()
-
     def g_terms(first, count, j):
         rows = [hscaled[sy, pl.ds(first, count)].reshape(count * 128, 512) for sy in range(2)]
         out = nn_dot(rows[0], dall[j, 0].reshape(512, 256))
@@ -630,6 +624,11 @@
         g_relay(j, 0).start()
     for j in range(2):
         g_relay(j, 1).start()
+    p_relay(0)
+    p_relay(1)
+    for n in range(7):
+        p_copy(1, n).start()
+
     for j in range(2):
         g_terms((za + (3, 1)[j]) % 4, 1, j)
         g_copy(j).start()
@@ -686,9 +685,12 @@
     for n in range(7):
         value = value + dots_in[n]
     sums[2] = value
-    for n in range(15):
+    mean_sibling.start()
+    g_relays(1)
+    mean_sibling.wait_recv()
+    sums[3] = sums[2] + sums_in[1, 0]
+    for n in range(7):
         mean_copy(n).start()
-    g_relays(1)
 
     owners(0)
     owners(1)
@@ -707,10 +709,10 @@
 
     wgrad_out = pltpu.make_async_copy(wgrad_ref, wgrad_hbm, isem.at[7])
     wgrad_out.start()
-    dot = sums[2]
-    for n in range(15):
+    dot = sums[3]
+    for n in range(7):
         mean_copy(n).wait_recv()
-        dot = dot + sums_in[1, n]
+        dot = dot + sums_in[1, 1 + n]
     factor = column_of(dot * (1.0 / 8192.0) / mean_square)
     inv_column = column_of(inv_root)
     for i in range(2):
@@ -747,8 +749,8 @@
     sq_sibling.wait_send()
     for n in range(7):
         sq_copy(n).wait_send()
-    for n in range(15):
         mean_copy(n).wait_send()
+    mean_sibling.wait_send()
     gram_copy.wait_send()
     for n in range(5):
         w_copy(n).wait_send()
@@ -825,8 +827,8 @@
             pltpu.VMEM((2, 4, 128, 512), BF16),
             pltpu.VMEM((2, 4, 128, 512), BF16),
             pltpu.VMEM((2, 4, 128, 256), BF16),
-            pltpu.VMEM((3, 1, 128), F32),
-            pltpu.VMEM((2, 15, 1, 128), F32),
+            pltpu.VMEM((4, 1, 128), F32),
+            pltpu.VMEM((2, 8, 1, 128), F32),
             pltpu.VMEM((2, 2, 2, 1, 128), F32),
             pltpu.VMEM((2, 2, 2, 1, 128), F32),
             pltpu.VMEM((7, 1, 128), F32),

time: 56.5 us -> 56.4 us (level)
  no operation moved by 1% of the time
where the time goes in v6:
time: 56.4 us; the launch traced here: 55.5 us
  Pallas kernels  54.8 us (97%)
  between operations  0.64 us (1%)
    pallas_call x1, Pallas kernels, shards(): pl.pallas_call(kernel, out_shape=(jax.ShapeDtypeStruct(hidden.shape, BF16...  53.2 us
    pallas_call x1, Pallas kernels, shards(): pl.pallas_call(hand_over, out_shape=tuple((jax.ShapeDtypeStruct(grad.shap...  1.66 us

profile of v6, /device:TPU:1, one launch (start us, length us, event | category | flops | bytes accessed | tf_op | source)
XLA Modules:
  0.0 55.5 jit_solution(9729341106434148619)
XLA Ops:
  0.6 53.2 %projection_backward.1 = (bf16[128,512]{1,0:T(8,128)(2,1)}, bf16[256,256]{1,0:T(8,128)(2,1)}) custom-call(bf16[128,512]{1,0:T(8,128)(2,1)} %hid_hbm.1, bf16[512]{0:T(512)(128)(2,1)} %gain_hbm.1, bf16[256,256]{1,0:T(8,128)(2,1)} %w_hbm.1, bf16[128,256]{1,0:T(8,128)(2,1)} %bc_hbm.1, bf16[128,1024]{1,0:T(8,128)(2,1)} %x_hbm.1, bf16[128,1024]{1,0:T(8,128)(2,1)} %dy_hbm.1, ...), custom_call_target="tpu_custom_call" | custom-call | tf_op jit(solution)/shard_map/projection_backward/pallas_call | solution.py:808
  53.8 1.7 %hand_over.1 = (bf16[128,512]{1,0:T(8,128)(2,1)}, bf16[256,256]{1,0:T(8,128)(2,1)}) custom-call(bf16[128,512]{1,0:T(8,128)(2,1)} %get-tuple-element.4.igrad_ref, bf16[256,256]{1,0:T(8,128)(2,1)} %get-tuple-element.5.wgrad_ref), custom_call_target="tpu_custom_call" | custom-call | tf_op jit(solution)/shard_map/hand_over/pallas_call | solution.py:855
